TPU v7x, 32 devices: a whole 2x2x4 slice. The times are simulated.
32 devices in a mesh: seq: 16 (over z, y, core), mp: 2 (over x).
Axes of the slice: x: 2, y: 2, z: 4, core: 2. Of those that a mesh axis runs over, the one named last changes fastest.
Arguments:
- tokens: bfloat16 [6144, 3072], P('seq', 'mp'), may hold values from -6 to 6
- w_qkv: bfloat16 [3072, 3, 3072], P(None, None, 'mp'), may hold values from -1 to 1
- q_gain: float32 [128], replicated, may hold values from 0 to 5
- k_gain: float32 [128], replicated, may hold values from 0 to 5
- w_out: bfloat16 [3072, 3072], P('mp'), may hold values from -0.15625 to 0.15625
- neighbours: int32 [16, 6], replicated, may hold values from 0 to 15, as said below
- counts: int32 [16], replicated, may hold values from 1 to 6
Outputs:
- mixed: bfloat16 [6144, 3072], P('seq', 'mp')
Inputs may be any that keep to these rules, and one draw needn't show every extreme that they name: `neighbours`: each row lists distinct tiles, each within 4 tiles of the row's own tile counted cyclically modulo 16.
All inputs are finite; a program needn't handle non-finite values.
Results may differ from a plain program's by a relative error of at most 0.014.
Values may be sent and summed in bfloat16 or wider, within the bound.
A program may use at most 192 MiB of HBM per device.

v0:
```python
import jax
import jax.numpy as jnp
from jax import lax
from jax.sharding import PartitionSpec as P

HD = 128
TILE = 384
REACH = 4
NB = 6


def passed_along(value, axis, steps):
    count = lax.axis_size(axis)
    pairs = [(source, (source + steps) % count) for source in range(count)]
    return lax.ppermute(value, axis, pairs)


def head_norm(projected, gain_vec):
    per_head = projected.reshape(projected.shape[0], -1, HD)
    factor = lax.rsqrt(jnp.mean(per_head * per_head, axis=-1, keepdims=True) + 1e-06)
    return (per_head * factor * gain_vec).astype(jnp.bfloat16)


def on_device(tokens, w_qkv, q_gain, k_gain, w_out, neighbours, counts):
    tok_rows = tokens.shape[0]
    columns = w_qkv.shape[2]
    heads_here = columns // HD
    tiles_here = tok_rows // TILE
    total_tiles = neighbours.shape[0]
    span_here = (REACH + tiles_here - 1) // tiles_here
    flat_w = w_qkv.reshape(w_qkv.shape[0], 3 * columns)
    projected = jnp.dot(
        lax.all_gather(tokens, "mp", axis=1, tiled=True), flat_w, preferred_element_type=jnp.float32
    )
    queries = head_norm(projected[:, :columns], q_gain)
    key_part = head_norm(projected[:, columns : 2 * columns], k_gain).reshape(tok_rows, columns)
    value_part = projected[:, 2 * columns :].astype(jnp.bfloat16)
    paired = jnp.stack([key_part, value_part])
    blocks = []
    for offset in range(-span_here, span_here + 1):
        if offset == 0:
            blocks.append(paired)
        else:
            blocks.append(passed_along(paired, "seq", -offset))
    window = jnp.concatenate(blocks, axis=1)
    window_tiles = (2 * span_here + 1) * tiles_here
    position = lax.axis_index("seq")
    first_tile = position * tiles_here - span_here * tiles_here
    listed = lax.dynamic_slice_in_dim(neighbours, position * tiles_here, tiles_here, 0)
    used_counts = lax.dynamic_slice_in_dim(counts, position * tiles_here, tiles_here, 0)
    relative = jnp.mod(listed - first_tile, total_tiles)
    slot_used = jnp.arange(NB, dtype=jnp.int32)[None, :] < used_counts[:, None]
    query_blocks = queries.reshape(tiles_here, TILE, heads_here, HD)
    factor = HD ** (-0.5)
    hits = (
        relative[:, :, None] == jnp.arange(window_tiles, dtype=jnp.int32)[None, None, :]
    ) & slot_used[:, :, None]
    tile_mask = jnp.any(hits, axis=1)
    key_mask = jnp.repeat(tile_mask, TILE, axis=1)
    near_keys = window[0].reshape(window_tiles * TILE, heads_here, HD)
    near_values = window[1].reshape(window_tiles * TILE, heads_here, HD)
    scores = (
        jnp.einsum("tqhd,khd->thqk", query_blocks, near_keys, preferred_element_type=jnp.float32)
        * factor
    )
    scores = jnp.where(key_mask[:, None, None, :], scores, -jnp.inf)
    highest = jnp.max(scores, axis=-1, keepdims=True)
    expo = jnp.exp(scores - highest)
    probs = (expo / jnp.sum(expo, axis=-1, keepdims=True)).astype(jnp.bfloat16)
    attended = jnp.einsum("thqk,khd->tqhd", probs, near_values, preferred_element_type=jnp.float32)
    attended = attended.astype(jnp.bfloat16).reshape(tok_rows, columns)
    mixed_t = lax.psum_scatter(
        lax.dot_general(
            w_out, attended, (((0,), (1,)), ((), ())), preferred_element_type=jnp.float32
        ).astype(jnp.bfloat16),
        "mp",
        scatter_dimension=0,
        tiled=True,
    ).astype(jnp.float32)
    return mixed_t.T.astype(jnp.bfloat16)


def solution(mesh):
    return jax.shard_map(
        on_device,
        mesh=mesh,
        in_specs=(P("seq", "mp"), P(None, None, "mp"), P(), P(), P("mp", None), P(), P()),
        out_specs=P("seq", "mp"),
        check_vma=False,
    )
```

profile of v0, /device:TPU:0, one launch (start us, length us, event | category | flops | bytes accessed | tf_op | source)
XLA Modules:
  0.0 529.9 jit_solution(3689720486348367093)
XLA Ops:
  6.5 0.0 copy-start
  6.5 0.7 all-gather.2.cloned.1.call-update
  7.3 0.0 reduce-scatter.2.cloned.1.call-start
  7.3 36.8 %copy.22 = bf16[3072,3,1536]{0,2,1:T(8,128)(2,1)} copy(bf16[3072,3,1536]{2,0,1:T(8,128)(2,1)} %param.8) | data formatting | bytes 56623104 | tf_op args[1]
  44.1 3.6 all-gather.2.cloned.1.call-done
  47.7 15.9 %fusion.21 = f32[384,4608]{1,0:T(8,128)S(1)} fusion(bf16[384,3072]{1,0:T(8,128)(2,1)} %all-gather.2.cloned.1.call-done, bf16[3072,4608]{0,1:T(8,128)(2,1)} %bitcast.62), kind=kOutput, calls=%fused_computation.47 | convolution fusion | flops 10871635968 | bytes 37748736 | tf_op jit(solution)/shard_map/dot_general | solution.py:32
  63.6 0.0 copy-start.4
  63.7 0.1 fusion.10
  63.8 2.8 copy-done.4
  66.6 1.8 slice_multiply_fusion
  68.3 2.0 copy.23
  70.4 0.7 reduce_sum.27
  71.1 0.7 add_rsqrt_fusion.1
  71.8 0.2 mul.67
  72.0 0.0 copy-start.10
  72.0 0.0 copy-start.9
  72.0 2.0 copy.24
  74.0 5.2 fusion.20
  79.2 1.6 pad_maximum_fusion
  80.8 1.5 collective-permute-start.2
  82.3 0.6 collective-permute-start.1
  82.9 1.5 collective-permute-start
  84.4 0.7 collective-permute-start.3
  85.1 3.8 collective-permute-start.4
  88.8 0.0 copy-done.10
  88.8 0.6 dynamic_slice.7
  89.5 0.2 fusion.14
  89.7 0.6 iota_compare_fusion.1
  90.3 47.6 %collective-permute-done.2 = bf16[2,384,1536]{2,1,0:T(8,128)(2,1)S(1)} collective-permute-done((bf16[2,384,1536]{2,1,0:T(8,128)(2,1)}, bf16[2,384,1536]{2,1,0:T(8,128)(2,1)S(1)}, u32[]{:S(2)}, u32[]{:S(2)}) %collective-permute-start.2) | collective-permute-done | bytes 2359328 | tf_op jit(solution)/shard_map/ppermute | solution.py:15
  137.9 1.5 collective-permute-start.5
  139.4 0.1 fusion.16
  139.5 0.1 broadcast_in_dim.12
  139.6 2.0 copy.27
  141.6 143.1 %collective-permute-done.1 = bf16[2,384,1536]{2,1,0:T(8,128)(2,1)} collective-permute-done((bf16[2,384,1536]{2,1,0:T(8,128)(2,1)}, bf16[2,384,1536]{2,1,0:T(8,128)(2,1)}, u32[]{:S(2)}, u32[]{:S(2)}) %collective-permute-start.1) | collective-permute-done | bytes 2359328 | tf_op jit(solution)/shard_map/ppermute | solution.py:15
  284.8 0.0 collective-permute-start.6
  284.8 0.2 multiply_reduce_fusion
  285.0 0.6 add_rsqrt_fusion
  285.6 0.0 collective-permute-done
  285.6 3.3 collective-permute-start.7
  288.9 1.8 constant_dynamic-update-slice_fusion.8
  290.7 1.8 constant_dynamic-update-slice_fusion.7
  292.6 0.2 constant_dynamic-update-slice_fusion.6
  292.7 0.0 collective-permute-done.3
  292.7 1.8 constant_dynamic-update-slice_fusion.5
  294.6 0.2 constant_dynamic-update-slice_fusion.4
  294.7 0.0 collective-permute-done.4
  294.7 1.8 constant_dynamic-update-slice_fusion.3
  296.6 0.0 collective-permute-done.5
  296.6 1.8 constant_dynamic-update-slice_fusion.2
  298.4 15.0 %collective-permute-done.6 = bf16[2,384,1536]{2,1,0:T(8,128)(2,1)S(1)} collective-permute-done((bf16[2,384,1536]{2,1,0:T(8,128)(2,1)}, bf16[2,384,1536]{2,1,0:T(8,128)(2,1)S(1)}, u32[]{:S(2)}, u32[]{:S(2)}) %collective-permute-start.6) | collective-permute-done | bytes 2359328 | tf_op jit(solution)/shard_map/ppermute | solution.py:15
  313.4 0.2 constant_dynamic-update-slice_fusion.1
  313.6 26.5 %collective-permute-done.7 = bf16[2,384,1536]{2,1,0:T(8,128)(2,1)S(1)} collective-permute-done((bf16[2,384,1536]{2,1,0:T(8,128)(2,1)}, bf16[2,384,1536]{2,1,0:T(8,128)(2,1)S(1)}, u32[]{:S(2)}, u32[]{:S(2)}) %collective-permute-start.7) | collective-permute-done | bytes 2359328 | tf_op jit(solution)/shard_map/ppermute | solution.py:15
  340.1 0.2 constant_dynamic-update-slice_fusion
  340.3 7.7 %fusion.19 = (bf16[1,3456,1536]{2,1,0:T(8,128)(2,1)}, bf16[1,3456,1536]{2,1,0:T(8,128)(2,1)}) fusion(bf16[2,3456,1536]{2,1,0:T(8,128)(2,1)S(1)} %constant_dynamic-update-slice_fusion), kind=kLoop, calls=%fused_computation.45 | loop fusion | bytes 42467328 | tf_op jit(solution)/shard_map/slice | solution.py:60
  348.0 13.8 %copy.26 = bf16[1,3456,1536]{1,2,0:T(8,128)(2,1)} copy(bf16[1,3456,1536]{2,1,0:T(8,128)(2,1)} %get-tuple-element.5) | data formatting | bytes 21233664 | tf_op jit(solution)/shard_map/slice | solution.py:60
  361.8 13.8 %copy.25 = bf16[1,3456,1536]{1,2,0:T(8,128)(2,1)} copy(bf16[1,3456,1536]{2,1,0:T(8,128)(2,1)} %get-tuple-element.6) | data formatting | bytes 21233664 | tf_op jit(solution)/shard_map/slice | solution.py:61
  375.6 0.0 copy-done.8
  375.6 28.2 %bitcast_reduce_fusion = (f32[12,384]{1,0:T(8,128)S(1)}, f32[12,3456,384]{2,1,0:T(8,128)}) fusion(pred[3456]{0:T(1024)(128)(4,1)S(1)} %broadcast_in_dim.13, bf16[3456,12,128]{0,2,1:T(8,128)(2,1)} %bitcast.61, f32[384,12,128]{0,2,1:T(8,128)S(1)} %bitcast.64, f32[128]{0:T(128)S(1)} %copy-done.8, f32[384,12]{0,1:T(8,128)S(1)} %copy-done.7), kind=kOutput, calls=%fused_computation.1 | convolution fusion | flops 4126404096 | bytes 76717952 | tf_op jit(solution)/shard_map/tqhd,khd->thqk/dot_general | solution.py:63
  403.8 20.4 %fusion.1 = f32[12,384]{1,0:T(8,128)S(1)} fusion(f32[12,3456,384]{2,1,0:T(8,128)} %get-tuple-element.10, f32[12,384]{1,0:T(8,128)S(1)} %get-tuple-element.9, pred[3456]{0:T(1024)(128)(4,1)S(1)} %broadcast_in_dim.13), kind=kLoop, calls=%fused_computation.5 | loop fusion | flops 63696384 | bytes 63741312 | tf_op jit(solution)/shard_map/reduce_sum | solution.py:69
  424.2 28.5 %fusion.5 = bf16[12,128,384]{2,1,0:T(8,128)(2,1)S(1)} fusion(bf16[3456,12,128]{0,2,1:T(8,128)(2,1)} %bitcast.65, f32[12,384]{1,0:T(8,128)S(1)} %fusion.1, f32[12,384]{1,0:T(8,128)S(1)} %get-tuple-element.9, f32[12,3456,384]{2,1,0:T(8,128)} %get-tuple-element.10, pred[3456]{0:T(1024)(128)(4,1)S(1)} %broadcast_in_dim.13), kind=kOutput, calls=%fused_computation.16 | convolution fusion | flops 4157079552 | bytes 75537792 | tf_op jit(solution)/shard_map/thqk,khd->tqhd/dot_general | solution.py:70
  452.7 0.0 copy-start.1
  452.7 8.9 %fusion.4 = bf16[3072,384]{0,1:T(8,128)(2,1)} fusion(bf16[384,1536]{0,1:T(8,128)(2,1)S(1)} %bitcast.68, bf16[1536,3072]{1,0:T(8,128)(2,1)} %param.11), kind=kOutput, calls=%fused_computation.9 | convolution fusion | flops 3625058304 | bytes 12976128 | tf_op jit(solution)/shard_map/dot_general | solution.py:73
  461.6 0.0 reduce-scatter.2.cloned.1.call-update
  461.7 61.4 %reduce-scatter.2.cloned.1.call-done = bf16[1536,384]{0,1:T(8,128)(2,1)} async-done(((bf16[3072,384]{0,1:T(8,128)(2,1)}), bf16[1536,384]{0,1:T(8,128)(2,1)}) %reduce-scatter.2.cloned.1.call-update) | async-done | bytes 1179664 | tf_op jit(solution)/shard_map/reduce_scatter | solution.py:72
  (17 shorter events, 0.0 us)
Async XLA Ops:
  6.5 37.6 %copy-start = (f32[128]{0:T(128)S(1)}, f32[128]{0:T(128)}, u32[]{:S(2)}) copy-start(f32[128]{0:T(128)} %param.10) | copy-start | bytes 1540
  6.5 41.2 %all-gather.2.cloned.1.call-start = ((), (), s32[]{:S(2)}) async-start(), calls=%async_computation.1 | async-start | bytes 3538944 | tf_op jit(solution)/shard_map/all_gather | solution.py:33
  7.3 515.8 %reduce-scatter.2.cloned.1.call-start = ((), (), s32[]{:S(2)}) async-start(), calls=%async_computation.2 | async-start | bytes 3538944 | tf_op jit(solution)/shard_map/reduce_scatter | solution.py:72
  63.6 2.9 copy-start.4
  66.6 12.6 %copy-start.2 = (bf16[1,384,1536]{2,1,0:T(8,128)(2,1)}, bf16[1,384,1536]{2,1,0:T(8,128)(2,1)S(1)}, u32[]{:S(2)}) copy-start(bf16[1,384,1536]{2,1,0:T(8,128)(2,1)S(1)} %fusion.10) | copy-start | bytes 3538948
  72.0 16.9 %copy-start.10 = (s32[16]{0:T(128)S(1)}, s32[16]{0:T(128)}, u32[]{:S(2)}) copy-start(s32[16]{0:T(128)} %param.13) | copy-start | bytes 196
  72.0 17.5 %copy-start.9 = (s32[16,6]{0,1:T(8,128)S(1)}, s32[16,6]{0,1:T(8,128)}, u32[]{:S(2)}) copy-start(s32[16,6]{0,1:T(8,128)} %param.12) | copy-start | bytes 1156
  80.8 57.1 %collective-permute-start.2 = (bf16[2,384,1536]{2,1,0:T(8,128)(2,1)}, bf16[2,384,1536]{2,1,0:T(8,128)(2,1)S(1)}, u32[]{:S(2)}, u32[]{:S(2)}) collective-permute-start(bf16[2,384,1536]{2,1,0:T(8,128)(2,1)} %pad_maximum_fusion), channel_id=1, source_target_pairs={{0,4},{2,6},{4,8},{6,10},{8,12},{10,14},{12,16},{14,18},{16,20},{1... | collective-permute-start | bytes 7077896 | tf_op jit(solution)/shard_map/ppermute | solution.py:15
  82.3 202.5 %collective-permute-start.1 = (bf16[2,384,1536]{2,1,0:T(8,128)(2,1)}, bf16[2,384,1536]{2,1,0:T(8,128)(2,1)}, u32[]{:S(2)}, u32[]{:S(2)}) collective-permute-start(bf16[2,384,1536]{2,1,0:T(8,128)(2,1)} %pad_maximum_fusion), channel_id=1, source_target_pairs={{0,6},{2,8},{4,10},{6,12},{8,14},{10,16},{12,18},{14,20},{16,22},{... | collective-permute-start | bytes 7077896 | tf_op jit(solution)/shard_map/ppermute | solution.py:15
  82.9 202.7 %collective-permute-start = (bf16[2,384,1536]{2,1,0:T(8,128)(2,1)}, bf16[2,384,1536]{2,1,0:T(8,128)(2,1)}, u32[]{:S(2)}, u32[]{:S(2)}) collective-permute-start(bf16[2,384,1536]{2,1,0:T(8,128)(2,1)} %pad_maximum_fusion), channel_id=1, source_target_pairs={{0,8},{2,10},{4,12},{6,14},{8,16},{10,18},{12,20},{14,22},{16,24},... | collective-permute-start | bytes 7077896 | tf_op jit(solution)/shard_map/ppermute | solution.py:15
  84.4 208.3 %collective-permute-start.3 = (bf16[2,384,1536]{2,1,0:T(8,128)(2,1)}, bf16[2,384,1536]{2,1,0:T(8,128)(2,1)}, u32[]{:S(2)}, u32[]{:S(2)}) collective-permute-start(bf16[2,384,1536]{2,1,0:T(8,128)(2,1)} %pad_maximum_fusion), channel_id=1, source_target_pairs={{0,2},{2,4},{4,6},{6,8},{8,10},{10,12},{12,14},{14,16},{16,18},{18... | collective-permute-start | bytes 7077896 | tf_op jit(solution)/shard_map/ppermute | solution.py:15
  85.1 209.7 %collective-permute-start.4 = (bf16[2,384,1536]{2,1,0:T(8,128)(2,1)}, bf16[2,384,1536]{2,1,0:T(8,128)(2,1)}, u32[]{:S(2)}, u32[]{:S(2)}) collective-permute-start(bf16[2,384,1536]{2,1,0:T(8,128)(2,1)} %pad_maximum_fusion), channel_id=1, source_target_pairs={{0,30},{2,0},{4,2},{6,4},{8,6},{10,8},{12,10},{14,12},{16,14},{18,... | collective-permute-start | bytes 7077896 | tf_op jit(solution)/shard_map/ppermute | solution.py:15
  137.9 1.7 copy-start.5
  137.9 158.7 %collective-permute-start.5 = (bf16[2,384,1536]{2,1,0:T(8,128)(2,1)}, bf16[2,384,1536]{2,1,0:T(8,128)(2,1)}, u32[]{:S(2)}, u32[]{:S(2)}) collective-permute-start(bf16[2,384,1536]{2,1,0:T(8,128)(2,1)} %pad_maximum_fusion), channel_id=1, source_target_pairs={{0,28},{2,30},{4,0},{6,2},{8,4},{10,6},{12,8},{14,10},{16,12},{18,... | collective-permute-start | bytes 7077896 | tf_op jit(solution)/shard_map/ppermute | solution.py:15
  141.6 150.9 %copy-start.6 = (bf16[2,384,1536]{2,1,0:T(8,128)(2,1)S(1)}, bf16[2,384,1536]{2,1,0:T(8,128)(2,1)}, u32[]{:S(2)}) copy-start(bf16[2,384,1536]{2,1,0:T(8,128)(2,1)} %copy-done.5) | copy-start | bytes 7077892
  284.8 28.6 %collective-permute-start.6 = (bf16[2,384,1536]{2,1,0:T(8,128)(2,1)}, bf16[2,384,1536]{2,1,0:T(8,128)(2,1)S(1)}, u32[]{:S(2)}, u32[]{:S(2)}) collective-permute-start(bf16[2,384,1536]{2,1,0:T(8,128)(2,1)} %pad_maximum_fusion), channel_id=1, source_target_pairs={{0,26},{2,28},{4,30},{6,0},{8,2},{10,4},{12,6},{14,8},{16,10},{18,... | collective-permute-start | bytes 7077896 | tf_op jit(solution)/shard_map/ppermute | solution.py:15
  285.6 9.0 %copy-start.3 = (bf16[1,384,1536]{2,1,0:T(8,128)(2,1)S(1)}, bf16[1,384,1536]{2,1,0:T(8,128)(2,1)}, u32[]{:S(2)}) copy-start(bf16[1,384,1536]{2,1,0:T(8,128)(2,1)} %copy-done.2) | copy-start | bytes 3538948
  285.6 54.5 %collective-permute-start.7 = (bf16[2,384,1536]{2,1,0:T(8,128)(2,1)}, bf16[2,384,1536]{2,1,0:T(8,128)(2,1)S(1)}, u32[]{:S(2)}, u32[]{:S(2)}) collective-permute-start(bf16[2,384,1536]{2,1,0:T(8,128)(2,1)} %pad_maximum_fusion), channel_id=1, source_target_pairs={{0,24},{2,26},{4,28},{6,30},{8,0},{10,2},{12,4},{14,6},{16,8},{18,... | collective-permute-start | bytes 7077896 | tf_op jit(solution)/shard_map/ppermute | solution.py:15
  361.8 13.8 %copy-start.7 = (f32[384,12]{0,1:T(8,128)S(1)}, f32[384,12]{0,1:T(8,128)}, u32[]{:S(2)}) copy-start(f32[384,12]{0,1:T(8,128)} %add_rsqrt_fusion) | copy-start | bytes 55300
  361.8 13.8 %copy-start.8 = (f32[128]{0:T(128)S(1)}, f32[128]{0:T(128)}, u32[]{:S(2)}) copy-start(f32[128]{0:T(128)} %param.9) | copy-start | bytes 1540
  452.7 70.3 %copy-start.1 = (f32[128]{0:T(128)S(1)}, f32[128]{0:T(128)}, u32[]{:S(2)}) copy-start(f32[128]{0:T(128)} %param.10) | copy-start | bytes 1540
Sparse Core Ops, SparseCore 0:
  8.9 38.7 all-gather.1
  461.8 61.2 reduce-scatter.1
where the time goes:
time: 532 us; the launch traced here: 530 us
  waiting for transfers between devices  298 us (56%)
  local copies, waits for them, and re-layouts  91.6 us (17%)
  matrix products  81.5 us (15%)
  other arithmetic  32.2 us (6%)
  between operations  13.6 us (3%)
  starting transfers between devices  12.9 us (2%)
    ppermute x8, waiting for transfers between devices, passed_along(): return lax.ppermute(value, axis, pairs)  232 us
    reduce_scatter x1, waiting for transfers between devices, on_device(): lax.psum_scatter(lax.dot_general(w_out, attended, (((0,), (1,)), ((), ())...  61.4 us
    unnamed x30, local copies, waits for them, and re-layouts  49 us
    dot_general x1, matrix products, on_device(): jnp.einsum('thqk,khd->tqhd', probs, near_values, preferred_element_type=j...  28.5 us
    dot_general x1, matrix products, on_device(): jnp.einsum('tqhd,khd->thqk', query_blocks, near_keys, preferred_element_t...  28.2 us
    slice x2, local copies, waits for them, and re-layouts, on_device(): near_keys = window[0].reshape(window_tiles * TILE, heads_here, HD)  21.5 us
    reduce_sum x1, other arithmetic, on_device(): probs = (expo / jnp.sum(expo, axis=-1, keepdims=True)).astype(jnp.bfloat16)  20.4 us
    dot_general x1, matrix products, on_device(): jnp.dot(lax.all_gather(tokens, 'mp', axis=1, tiled=True), flat_w, preferr...  15.9 us
  transfers between devices with their start and end apart: 10, of which 6 were waited for; matrix products, arithmetic and copies ran while one was open for 10% of the time, Pallas kernels for 0%

commit v1 on v0

v1 whole, which is shorter than its diff:
```python
import functools

import jax
import jax.numpy as jnp
from jax import lax
from jax.experimental import pallas as pl
from jax.experimental.pallas import tpu as pltpu
from jax.sharding import PartitionSpec as P

HD = 128
TILE = 384
EPS = 1e-06
LOG2E = 1.4426950408889634
VMEM = 48 * 1024 * 1024


def width_of(columns):
    return 256 if columns % 256 == 0 else 128


def normed(product, gain):
    parts = []
    for first in range(0, product.shape[1], HD):
        head = product[:, first : first + HD]
        factor = lax.rsqrt(jnp.mean(head * head, axis=-1, keepdims=True) + EPS)
        parts.append(head * factor * gain)
    return parts[0] if len(parts) == 1 else jnp.concatenate(parts, axis=1)


def project_kernel(low_ref, high_ref, w_ref, gain_ref, out_ref):
    half = low_ref.shape[1]
    product = jnp.dot(low_ref[...], w_ref[0, :half, :], preferred_element_type=jnp.float32)
    product += jnp.dot(high_ref[...], w_ref[0, half:, :], preferred_element_type=jnp.float32)

    @pl.when(pl.program_id(0) == 0)
    def _():
        out_ref[0] = normed(product, gain_ref[...]).astype(out_ref.dtype)

    @pl.when(pl.program_id(0) != 0)
    def _():
        out_ref[0] = product.astype(out_ref.dtype)


def project(low, high, w, gain, kind, kinds, first_col, columns):
    rows, half = low.shape
    depth = w.shape[1]
    wide = width_of(columns)
    base = first_col // wide
    return pl.pallas_call(
        project_kernel,
        grid=(kinds, columns // wide),
        in_specs=[
            pl.BlockSpec((rows, half), lambda i, j: (0, 0)),
            pl.BlockSpec((rows, half), lambda i, j: (0, 0)),
            pl.BlockSpec((1, depth, wide), lambda i, j: (kind + i, 0, base + j)),
            pl.BlockSpec((1, HD), lambda i, j: (0, 0)),
        ],
        out_specs=pl.BlockSpec((1, rows, wide), lambda i, j: (i, 0, j)),
        out_shape=jax.ShapeDtypeStruct((kinds, rows, columns), jnp.bfloat16),
        compiler_params=pltpu.CompilerParams(vmem_limit_bytes=VMEM),
        cost_estimate=pl.CostEstimate(
            flops=2 * rows * depth * columns * kinds,
            bytes_accessed=2 * depth * columns * kinds + 2 * rows * (depth + columns * kinds),
            transcendentals=0,
        ),
        name="project",
    )(low, high, w, gain)


def attend_kernel(used_ref, q_ref, *refs):
    blocks = refs[:9]
    out_ref, top, total, acc = refs[9:]
    top[...] = jnp.full(top.shape, -jnp.inf, jnp.float32)
    total[...] = jnp.zeros(total.shape, jnp.float32)
    acc[...] = jnp.zeros(acc.shape, jnp.float32)
    scale = HD ** (-0.5) * LOG2E
    for index, block in enumerate(blocks):

        @pl.when(used_ref[index] != 0)
        def _(block=block):
            scores = lax.dot_general(
                block[0], q_ref[0], (((1,), (1,)), ((), ())), preferred_element_type=jnp.float32
            ) * scale
            before = top[...]
            now = jnp.maximum(before, jnp.max(scores, axis=0, keepdims=True))
            shrink = jnp.exp2(before - now)
            expo = jnp.exp2(scores - now)
            top[...] = now
            total[...] = total[...] * shrink + jnp.sum(expo, axis=0, keepdims=True)
            acc[...] = acc[...] * shrink + lax.dot_general(
                block[1],
                expo.astype(jnp.bfloat16),
                (((0,), (0,)), ((), ())),
                preferred_element_type=jnp.float32,
            )

    out_ref[...] = (acc[...] / total[...]).T.astype(out_ref.dtype)


def attend(used, queries, blocks, first_col, columns):
    rows = queries.shape[1]
    base = first_col // HD
    heads = columns // HD
    pair = pl.BlockSpec((2, rows, HD), lambda h, used: (0, 0, h))
    return pl.pallas_call(
        attend_kernel,
        grid_spec=pltpu.PrefetchScalarGridSpec(
            num_scalar_prefetch=1,
            grid=(heads,),
            in_specs=[pl.BlockSpec((1, rows, HD), lambda h, used: (0, 0, base + h))] + [pair] * 9,
            out_specs=pl.BlockSpec((rows, HD), lambda h, used: (0, h)),
            scratch_shapes=[
                pltpu.VMEM((1, rows), jnp.float32),
                pltpu.VMEM((1, rows), jnp.float32),
                pltpu.VMEM((HD, rows), jnp.float32),
            ],
        ),
        out_shape=jax.ShapeDtypeStruct((rows, columns), jnp.bfloat16),
        compiler_params=pltpu.CompilerParams(vmem_limit_bytes=VMEM),
        cost_estimate=pl.CostEstimate(
            flops=4 * rows * rows * 9 * columns,
            bytes_accessed=2 * rows * columns * 20,
            transcendentals=9 * rows * rows * heads,
        ),
        name="attend",
    )(used, queries, *blocks)


def mix_kernel(chunks, side_ref, *refs):
    own, other = refs[:chunks], refs[chunks : 2 * chunks]
    w_own, w_low, w_high, out_ref = refs[2 * chunks :]
    columns = own[0].shape[1]
    half = w_low.shape[0]
    product = jnp.zeros(out_ref.shape, jnp.float32)
    mine = jnp.concatenate([piece[...] for piece in own], axis=1)
    theirs = jnp.concatenate([piece[...] for piece in other], axis=1)
    product = jnp.dot(mine, w_own[...], preferred_element_type=jnp.float32)
    product += jnp.dot(theirs[:, :half], w_low[...], preferred_element_type=jnp.float32)
    product += jnp.dot(theirs[:, half:], w_high[...], preferred_element_type=jnp.float32)
    out_ref[...] = product.astype(out_ref.dtype)


def mix(side, own, other, w_out, w_low, w_high):
    rows, columns = own[0].shape
    depth = w_out.shape[0]
    width = w_low.shape[1]
    wide = width_of(width)
    steps = width // wide
    piece = pl.BlockSpec((rows, columns), lambda j, side: (0, 0))
    half = pl.BlockSpec((depth // 2, wide), lambda j, side: (0, j))
    return pl.pallas_call(
        functools.partial(mix_kernel, len(own)),
        grid_spec=pltpu.PrefetchScalarGridSpec(
            num_scalar_prefetch=1,
            grid=(steps,),
            in_specs=[piece] * (2 * len(own))
            + [pl.BlockSpec((depth, wide), lambda j, side: (0, side[0] * steps + j)), half, half],
            out_specs=pl.BlockSpec((rows, wide), lambda j, side: (0, j)),
        ),
        out_shape=jax.ShapeDtypeStruct((rows, width), jnp.bfloat16),
        compiler_params=pltpu.CompilerParams(vmem_limit_bytes=VMEM),
        cost_estimate=pl.CostEstimate(
            flops=4 * rows * depth * width, bytes_accessed=4 * depth * width, transcendentals=0
        ),
        name="mix",
    )(side, *own, *other, w_out, w_low, w_high)


def shifted(value, axis, target):
    count = lax.axis_size(axis)
    return lax.ppermute(value, axis, [(s, target(s) % count) for s in range(count)])


def on_device(tokens, w_qkv, q_gain, k_gain, w_out, neighbours, counts):
    columns = w_qkv.shape[2]
    heads_here = columns // HD
    total_tiles = neighbours.shape[0]
    sides = lax.axis_size("mp")
    side = lax.axis_index("mp")
    tile = lax.axis_index("seq")
    core, row = tile % 2, (tile // 2) % 2
    parts = 3 if heads_here % 3 == 0 else 1
    part_cols = columns // parts

    w = jnp.transpose(w_qkv, (1, 0, 2))
    q_gain, k_gain = q_gain.reshape(1, HD), k_gain.reshape(1, HD)

    if sides == 2:
        across = shifted(tokens, "mp", lambda s: s + 1)
        low = jnp.where(side == 0, tokens, across)
        high = jnp.where(side == 0, across, tokens)
    else:
        across = lax.all_gather(tokens, "mp", axis=1, tiled=True)
        low, high = jnp.split(across, 2, axis=1)

    turn = jnp.where(row == 0, -4, 4)
    spin = jnp.where(core == 0, -4, 4)
    held = jnp.stack(
        [tile, tile - 4, tile + 4, tile ^ 2, (tile ^ 2) + turn,
         tile ^ 1, (tile ^ 1) + spin, tile ^ 3, (tile ^ 3) + turn]
    )
    held = jnp.mod(held, total_tiles)
    listed = lax.dynamic_index_in_dim(neighbours, tile, 0, keepdims=False)
    in_use = jnp.arange(listed.shape[0], dtype=jnp.int32) < counts[tile]
    used = jnp.any((held[:, None] == listed[None, :]) & in_use[None, :], axis=1).astype(jnp.int32)

    windows = []
    for part in range(parts):
        own = project(low, high, w, k_gain, 1, 2, part * part_cols, part_cols)
        below = shifted(own, "seq", lambda s: s + 4)
        above = shifted(own, "seq", lambda s: s - 4)
        beside = shifted(own, "seq", lambda s: s ^ 2)
        twin = shifted(own, "seq", lambda s: s ^ 1)
        beyond = shifted(jnp.where(row == 1, below, above), "seq", lambda s: s ^ 2)
        twin_far = shifted(jnp.where(core == 1, below, above), "seq", lambda s: s ^ 1)
        twin_beside = shifted(beside, "seq", lambda s: s ^ 1)
        twin_beyond = shifted(beyond, "seq", lambda s: s ^ 1)
        windows.append(
            [own, below, above, beside, beyond, twin, twin_far, twin_beside, twin_beyond]
        )
    queries = project(low, high, w, q_gain, 0, 1, 0, columns)

    if sides == 2:
        depth, width = w_out.shape[0] // 2, w_out.shape[1] // 2
        sent = lax.dynamic_slice(w_out, (core * depth, (1 - side) * width), (depth, width))
        sent, _ = lax.optimization_barrier((sent, across))
        got = shifted(sent, "mp", lambda s: s + 1)
        got_twin = shifted(got, "seq", lambda s: s ^ 1)
        w_low = jnp.where(core == 0, got, got_twin)
        w_high = jnp.where(core == 0, got_twin, got)

    attended = [
        attend(used, queries, windows[part], part * part_cols, part_cols) for part in range(parts)
    ]
    if sides == 2:
        other = [shifted(piece, "mp", lambda s: s + 1) for piece in attended]
        return mix(side.reshape(1).astype(jnp.int32), attended, other, w_out, w_low, w_high)
    terms = jnp.dot(
        jnp.concatenate(attended, axis=1), w_out, preferred_element_type=jnp.float32
    ).astype(jnp.bfloat16)
    return lax.psum_scatter(terms, "mp", scatter_dimension=1, tiled=True)


def solution(mesh):
    return jax.shard_map(
        on_device,
        mesh=mesh,
        in_specs=(P("seq", "mp"), P(None, None, "mp"), P(), P(), P("mp", None), P(), P()),
        out_specs=P("seq", "mp"),
        check_vma=False,
    )
```

time: 532 us -> 262 us (0.49)
  waiting for transfers between devices: 298 us -> 105 us
  Pallas kernels: 0 us -> 84.4 us
  local copies, waits for them, and re-layouts: 91.6 us -> 9.83 us
  matrix products: 81.5 us -> 0 us
  starting transfers between devices: 12.9 us -> 51.1 us
  other arithmetic: 32.2 us -> 10.5 us
  between operations: 13.6 us -> 0.24 us
    ppermute x8 -> x30, waiting for transfers between devices: 232 us -> 105 us  [shifted(): lax.ppermute(value, axis, [(s, target(s) % count) for s in range(count)])]
    pallas_call x0 -> x8, Pallas kernels: none -> 84.4 us  [the longest x3 49.5 us: attend(): pl.pallas_call(attend_kernel, grid_spec=pltpu.PrefetchScalarGridSpec(num_...]
    dot_general x4 -> x0, matrix products: 81.5 us -> none  [the longest x1 28.5 us: on_device(): jnp.einsum('thqk,khd->tqhd', probs, near_values, preferred_element_type=j...]
    reduce_scatter x1 -> x0, waiting for transfers between devices: 61.4 us -> none  [on_device(): lax.psum_scatter(lax.dot_general(w_out, attended, (((0,), (1,)), ((), ())...]
    unnamed x30 -> x42, local copies, waits for them, and re-layouts: 49 us -> 5.71 us
    ppermute x8 -> x30, starting transfers between devices: 12.9 us -> 51.1 us  [shifted(): lax.ppermute(value, axis, [(s, target(s) % count) for s in range(count)])]
    slice x4 -> x0, local copies, waits for them, and re-layouts: 37.4 us -> none  [the longest x2 21.5 us: on_device(): near_keys = window[0].reshape(window_tiles * TILE, heads_here, HD)]
    reduce_sum x3 -> x0, other arithmetic: 21.3 us -> none  [the longest x1 20.4 us: on_device(): probs = (expo / jnp.sum(expo, axis=-1, keepdims=True)).astype(jnp.bfloat16)]
  transfers between devices with their start and end apart: 10 -> 30, of which waited for: 6 -> 11; matrix products, arithmetic and copies ran while one was open for 10% -> 5% of each run, Pallas kernels for 0% -> 27%
where the time goes in v1:
time: 262 us; the launch traced here: 261 us
  waiting for transfers between devices  105 us (40%)
  Pallas kernels  84.4 us (32%)
  starting transfers between devices  51.1 us (20%)
  other arithmetic  10.5 us (4%)
  local copies, waits for them, and re-layouts  9.83 us (4%)
    ppermute x30, waiting for transfers between devices, shifted(): lax.ppermute(value, axis, [(s, target(s) % count) for s in range(count)])  105 us
    ppermute x30, starting transfers between devices, shifted(): lax.ppermute(value, axis, [(s, target(s) % count) for s in range(count)])  51.1 us
    pallas_call x3, Pallas kernels, attend(): pl.pallas_call(attend_kernel, grid_spec=pltpu.PrefetchScalarGridSpec(num_...  49.5 us
    pallas_call x4, Pallas kernels, project(): pl.pallas_call(project_kernel, grid=(kinds, columns // wide), in_specs=[p...  27 us
    pallas_call x1, Pallas kernels, mix(): pl.pallas_call(functools.partial(mix_kernel, len(own)), grid_spec=pltpu.P...  7.95 us
    unnamed x42, local copies, waits for them, and re-layouts  5.71 us
  transfers between devices with their start and end apart: 30, of which 11 were waited for; matrix products, arithmetic and copies ran while one was open for 5% of the time, Pallas kernels for 27%

profile of v1, /device:TPU:0, one launch (start us, length us, event | category | flops | bytes accessed | tf_op | source)
XLA Modules:
  0.0 260.8 jit_solution(15298716885474916572)
XLA Ops:
  0.0 2.9 %collective-permute-start = (bf16[384,1536]{1,0:T(8,128)(2,1)}, bf16[384,1536]{1,0:T(8,128)(2,1)}, u32[]{:S(2)}, u32[]{:S(2)}) collective-permute-start(bf16[384,1536]{1,0:T(8,128)(2,1)} %param.7), channel_id=1, source_target_pairs={{0,1},{1,0},{2,3},{3,2},{4,5},{5,4},{6,7},{7,6},{8,9},{9,8},{10,11... | collective-permute-start | bytes 3538952 | tf_op jit(solution)/shard_map/ppermute | solution.py:171
  2.9 26.3 %collective-permute-done = bf16[384,1536]{1,0:T(8,128)(2,1)} collective-permute-done((bf16[384,1536]{1,0:T(8,128)(2,1)}, bf16[384,1536]{1,0:T(8,128)(2,1)}, u32[]{:S(2)}, u32[]{:S(2)}) %collective-permute-start) | collective-permute-done | bytes 1179680 | tf_op jit(solution)/shard_map/ppermute | solution.py:171
  29.2 1.8 broadcast_select_fusion.2
  31.0 6.5 %project.5.refs_0_ = bf16[2,384,512]{2,1,0:T(8,128)(2,1)} custom-call(bf16[384,1536]{1,0:T(8,128)(2,1)S(1)} %get-tuple-element.10.low_ref, bf16[384,1536]{1,0:T(8,128)(2,1)S(1)} %get-tuple-element.9.high_ref, bf16[3,3072,1536]{2,1,0:T(8,128)(2,1)} %bitcast.18, f32[1,128]{1,0:T(1,128)S(1)} %bitcast.14), custom_call_target="tpu_custom_call" | custom-call | flops 2415919104 | bytes 9437184 | tf_op jit(solution)/shard_map/project/pallas_call | solution.py:49
  37.5 1.8 collective-permute-start.1
  39.4 2.0 collective-permute-start.2
  41.4 1.7 collective-permute-start.3
  43.1 0.0 collective-permute-start.5
  43.1 3.3 %dynamic_slice.12 = bf16[768,1536]{1,0:T(8,128)(2,1)} dynamic-slice(bf16[1536,3072]{1,0:T(8,128)(2,1)} %refs_6_.1, s32[]{:T(128)S(6)} %select_n.116, s32[]{:T(128)S(6)} %select_n.117), dynamic_slice_sizes={768,1536} | dynamic-slice | bytes 4718596 | tf_op jit(solution)/shard_map/dynamic_slice | solution.py:225
  46.4 1.5 collective-permute-start.28
  47.9 6.5 %project.6.refs_0_ = bf16[2,384,512]{2,1,0:T(8,128)(2,1)} custom-call(bf16[384,1536]{1,0:T(8,128)(2,1)S(1)} %get-tuple-element.10.low_ref, bf16[384,1536]{1,0:T(8,128)(2,1)S(1)} %get-tuple-element.9.high_ref, bf16[3,3072,1536]{2,1,0:T(8,128)(2,1)} %bitcast.19, f32[1,128]{1,0:T(1,128)S(1)} %bitcast.15), custom_call_target="tpu_custom_call" | custom-call | flops 2415919104 | bytes 9437184 | tf_op jit(solution)/shard_map/project/pallas_call | solution.py:49
  54.4 5.7 %collective-permute-done.1.refs_1_ = bf16[2,384,512]{2,1,0:T(8,128)(2,1)S(1)} collective-permute-done((bf16[2,384,512]{2,1,0:T(8,128)(2,1)}, bf16[2,384,512]{2,1,0:T(8,128)(2,1)S(1)}, u32[]{:S(2)}, u32[]{:S(2)}) %collective-permute-start.1) | collective-permute-done | bytes 786464 | tf_op jit(solution)/shard_map/ppermute | solution.py:171
  60.1 12.4 %collective-permute-start.9 = (bf16[2,384,512]{2,1,0:T(8,128)(2,1)}, bf16[2,384,512]{2,1,0:T(8,128)(2,1)}, u32[]{:S(2)}, u32[]{:S(2)}) collective-permute-start(bf16[2,384,512]{2,1,0:T(8,128)(2,1)} %project.6.refs_0_), channel_id=1, source_target_pairs={{0,8},{2,10},{4,12},{6,14},{8,16},{10,18},{12,20},{14,22},{16,24},... | collective-permute-start | bytes 2359304 | tf_op jit(solution)/shard_map/ppermute | solution.py:171
  72.5 3.3 %collective-permute-done.2.refs_2_ = bf16[2,384,512]{2,1,0:T(8,128)(2,1)} collective-permute-done((bf16[2,384,512]{2,1,0:T(8,128)(2,1)}, bf16[2,384,512]{2,1,0:T(8,128)(2,1)}, u32[]{:S(2)}, u32[]{:S(2)}) %collective-permute-start.2) | collective-permute-done | bytes 786464 | tf_op jit(solution)/shard_map/ppermute | solution.py:171
  75.8 3.0 %collective-permute-start.10 = (bf16[2,384,512]{2,1,0:T(8,128)(2,1)}, bf16[2,384,512]{2,1,0:T(8,128)(2,1)}, u32[]{:S(2)}, u32[]{:S(2)}) collective-permute-start(bf16[2,384,512]{2,1,0:T(8,128)(2,1)} %project.6.refs_0_), channel_id=1, source_target_pairs={{0,24},{2,26},{4,28},{6,30},{8,0},{10,2},{12,4},{14,6},{16,8},{18,... | collective-permute-start | bytes 2359304 | tf_op jit(solution)/shard_map/ppermute | solution.py:171
  78.9 1.5 collective-permute-start.11
  80.4 5.8 %project.7.refs_0_ = bf16[2,384,512]{2,1,0:T(8,128)(2,1)S(1)} custom-call(bf16[384,1536]{1,0:T(8,128)(2,1)S(1)} %get-tuple-element.10.low_ref, bf16[384,1536]{1,0:T(8,128)(2,1)S(1)} %get-tuple-element.9.high_ref, bf16[3,3072,1536]{2,1,0:T(8,128)(2,1)} %bitcast.20, f32[1,128]{1,0:T(1,128)S(1)} %bitcast.16), custom_call_target="tpu_custom_call" | custom-call | flops 2415919104 | bytes 9437184 | tf_op jit(solution)/shard_map/project/pallas_call | solution.py:49
  86.2 8.6 %collective-permute-done.9.refs_1_ = bf16[2,384,512]{2,1,0:T(8,128)(2,1)} collective-permute-done((bf16[2,384,512]{2,1,0:T(8,128)(2,1)}, bf16[2,384,512]{2,1,0:T(8,128)(2,1)}, u32[]{:S(2)}, u32[]{:S(2)}) %collective-permute-start.9) | collective-permute-done | bytes 786464 | tf_op jit(solution)/shard_map/ppermute | solution.py:171
  94.8 12.4 %collective-permute-start.17 = (bf16[2,384,512]{2,1,0:T(8,128)(2,1)S(1)}, bf16[2,384,512]{2,1,0:T(8,128)(2,1)S(1)}, u32[]{:S(2)}, u32[]{:S(2)}) collective-permute-start(bf16[2,384,512]{2,1,0:T(8,128)(2,1)S(1)} %project.7.refs_0_), channel_id=1, source_target_pairs={{0,8},{2,10},{4,12},{6,14},{8,16},{10,18},{12,20},{14,22},{16,24},... | collective-permute-start | bytes 2359304 | tf_op jit(solution)/shard_map/ppermute | solution.py:171
  107.2 1.2 broadcast_select_fusion.6
  108.4 3.1 %collective-permute-done.10.refs_2_ = bf16[2,384,512]{2,1,0:T(8,128)(2,1)} collective-permute-done((bf16[2,384,512]{2,1,0:T(8,128)(2,1)}, bf16[2,384,512]{2,1,0:T(8,128)(2,1)}, u32[]{:S(2)}, u32[]{:S(2)}) %collective-permute-start.10) | collective-permute-done | bytes 786464 | tf_op jit(solution)/shard_map/ppermute | solution.py:171
  111.5 1.1 collective-permute-start.18
  112.6 1.5 collective-permute-start.19
  114.1 0.5 collective-permute-start.4
  114.6 1.5 broadcast_select_fusion.5
  116.1 0.0 copy-start.20
  116.1 0.0 copy-start.10
  116.2 13.3 %collective-permute-done.17.refs_1_ = bf16[2,384,512]{2,1,0:T(8,128)(2,1)S(1)} collective-permute-done((bf16[2,384,512]{2,1,0:T(8,128)(2,1)S(1)}, bf16[2,384,512]{2,1,0:T(8,128)(2,1)S(1)}, u32[]{:S(2)}, u32[]{:S(2)}) %collective-permute-start.17) | collective-permute-done | bytes 786464 | tf_op jit(solution)/shard_map/ppermute | solution.py:171
  129.5 13.1 %collective-permute-done.18.refs_2_ = bf16[2,384,512]{2,1,0:T(8,128)(2,1)S(1)} collective-permute-done((bf16[2,384,512]{2,1,0:T(8,128)(2,1)S(1)}, bf16[2,384,512]{2,1,0:T(8,128)(2,1)S(1)}, u32[]{:S(2)}, u32[]{:S(2)}) %collective-permute-start.18) | collective-permute-done | bytes 786464 | tf_op jit(solution)/shard_map/ppermute | solution.py:171
  142.6 0.1 collective-permute-start.7
  142.7 1.5 collective-permute-start.12
  144.3 5.5 %collective-permute-done.4.refs_4_ = bf16[2,384,512]{2,1,0:T(8,128)(2,1)} collective-permute-done((bf16[2,384,512]{2,1,0:T(8,128)(2,1)S(1)}, bf16[2,384,512]{2,1,0:T(8,128)(2,1)}, u32[]{:S(2)}, u32[]{:S(2)}) %collective-permute-start.4) | collective-permute-done | bytes 786464 | tf_op jit(solution)/shard_map/ppermute | solution.py:171
  149.8 0.5 collective-permute-start.29
  150.3 1.2 broadcast_select_fusion.4
  151.6 0.9 copy-done.3
  152.5 0.9 copy-done.13
  153.4 0.0 collective-permute-start.15
  153.4 1.6 collective-permute-start.20
  155.0 11.7 %collective-permute-done.12.refs_4_ = bf16[2,384,512]{2,1,0:T(8,128)(2,1)} collective-permute-done((bf16[2,384,512]{2,1,0:T(8,128)(2,1)S(1)}, bf16[2,384,512]{2,1,0:T(8,128)(2,1)}, u32[]{:S(2)}, u32[]{:S(2)}) %collective-permute-start.12) | collective-permute-done | bytes 786464 | tf_op jit(solution)/shard_map/ppermute | solution.py:171
  166.7 0.9 copy-done.15
  167.6 0.5 collective-permute-start.16
  168.1 0.2 dynamic-slice_reduce_fusion
  168.3 0.6 dynamic_slice.11
  168.9 0.1 stack.39
  169.0 0.6 iota_compare_fusion
  169.5 0.1 and_reduce_fusion
  169.7 0.1 collective-permute-start.21
  169.7 11.8 %collective-permute-done.20.refs_4_ = bf16[2,384,512]{2,1,0:T(8,128)(2,1)} collective-permute-done((bf16[2,384,512]{2,1,0:T(8,128)(2,1)}, bf16[2,384,512]{2,1,0:T(8,128)(2,1)}, u32[]{:S(2)}, u32[]{:S(2)}) %collective-permute-start.20) | collective-permute-done | bytes 786464 | tf_op jit(solution)/shard_map/ppermute | solution.py:171
  181.6 0.5 collective-permute-start.23
  182.1 0.1 collective-permute-start.24
  182.2 8.2 %project.4.q_ref = bf16[1,384,1536]{2,1,0:T(8,128)(2,1)S(1)} custom-call(bf16[384,1536]{1,0:T(8,128)(2,1)S(1)} %get-tuple-element.10.low_ref, bf16[384,1536]{1,0:T(8,128)(2,1)S(1)} %get-tuple-element.9.high_ref, bf16[3,3072,1536]{2,1,0:T(8,128)(2,1)} %bitcast.21, f32[1,128]{1,0:T(1,128)S(1)} %bitcast.17), custom_call_target="tpu_custom_call" | custom-call | flops 3623878656 | bytes 12976128 | tf_op jit(solution)/shard_map/project/pallas_call | solution.py:49
  190.3 0.0 copy-start.2
  190.4 1.0 copy-done.2
  191.4 16.4 %attend.3.refs_0_ = bf16[384,512]{1,0:T(8,128)(2,1)S(1)} custom-call(s32[9]{0:T(128)S(1)} %convert_element_type.3.used_ref, bf16[1,384,1536]{2,1,0:T(8,128)(2,1)} %copy-done.2, bf16[2,384,512]{2,1,0:T(8,128)(2,1)} %project.5.refs_0_, bf16[2,384,512]{2,1,0:T(8,128)(2,1)S(1)} %collective-permute-done.1.refs_1_, ...), custom_call_target="tpu_custom_call" | custom-call | flops 2717908992 | bytes 7864320 | tf_op jit(solution)/shard_map/attend/pallas_call | solution.py:105
  207.8 16.7 %attend.4.refs_1_ = bf16[384,512]{1,0:T(8,128)(2,1)S(1)} custom-call(s32[9]{0:T(128)S(1)} %convert_element_type.3.used_ref, bf16[1,384,1536]{2,1,0:T(8,128)(2,1)} %copy-done.2, bf16[2,384,512]{2,1,0:T(8,128)(2,1)} %project.6.refs_0_, bf16[2,384,512]{2,1,0:T(8,128)(2,1)} %collective-permute-done.9.refs_1_, ...), custom_call_target="tpu_custom_call" | custom-call | flops 2717908992 | bytes 7864320 | tf_op jit(solution)/shard_map/attend/pallas_call | solution.py:105
  224.5 1.6 collective-permute-start.25
  226.0 0.5 collective-permute-start.26
  226.6 0.9 copy-done.18
  227.5 1.0 copy-done.19
  228.5 16.4 %attend.5.refs_2_ = bf16[384,512]{1,0:T(8,128)(2,1)S(1)} custom-call(s32[9]{0:T(128)S(1)} %convert_element_type.3.used_ref, bf16[1,384,1536]{2,1,0:T(8,128)(2,1)} %copy-done.2, bf16[2,384,512]{2,1,0:T(8,128)(2,1)S(1)} %copy-done.8, bf16[2,384,512]{2,1,0:T(8,128)(2,1)S(1)} %copy-done.4, bf16[2,384,512]{2,1,0:T(8,128)(2,1)S(1)} %copy-done.6, ...), custom_call_target="tpu_custom_call" | custom-call | flops 2717908992 | bytes 7864320 | tf_op jit(solution)/shard_map/attend/pallas_call | solution.py:105
  245.0 1.6 collective-permute-start.27
  246.5 4.1 %broadcast_select_fusion = (bf16[768,1536]{1,0:T(8,128)(2,1)}, bf16[768,1536]{1,0:T(8,128)(2,1)S(1)}) fusion(bf16[768,1536]{1,0:T(8,128)(2,1)} %collective-permute-done.29, bf16[768,1536]{1,0:T(8,128)(2,1)} %collective-permute-done.28, pred[]{:T(512)S(6)} %eq.43), kind=kLoop, calls=%fused_computation | loop fusion | flops 2359296 | bytes 9437185 | tf_op jit(solution)/shard_map/jit(_where)/select_n | solution.py:230
  250.6 2.2 collective-permute-done.27.refs_5_
  252.8 7.9 %mix.1 = bf16[384,1536]{1,0:T(8,128)(2,1)} custom-call(s32[1]{0:T(128)} %bitcast.side_ref, bf16[384,512]{1,0:T(8,128)(2,1)S(1)} %attend.3.refs_0_, bf16[384,512]{1,0:T(8,128)(2,1)S(1)} %attend.4.refs_1_, bf16[384,512]{1,0:T(8,128)(2,1)S(1)} %attend.5.refs_2_, bf16[384,512]{1,0:T(8,128)(2,1)S(1)} %collective-permute-done.25.refs_3_, ...), custom_call_target="tpu_custom_call" | custom-call | flops 3623878656 | bytes 9437184 | tf_op jit(solution)/shard_map/mix/pallas_call | solution.py:151
  (59 shorter events, 0.1 us)
Async XLA Ops:
  0.0 168.1 %copy-start = (s32[16,6]{0,1:T(8,128)S(1)}, s32[16,6]{0,1:T(8,128)}, u32[]{:S(2)}) copy-start(s32[16,6]{0,1:T(8,128)} %param.12) | copy-start | bytes 1156
  0.0 29.2 %collective-permute-start = (bf16[384,1536]{1,0:T(8,128)(2,1)}, bf16[384,1536]{1,0:T(8,128)(2,1)}, u32[]{:S(2)}, u32[]{:S(2)}) collective-permute-start(bf16[384,1536]{1,0:T(8,128)(2,1)} %param.7), channel_id=1, source_target_pairs={{0,1},{1,0},{2,3},{3,2},{4,5},{5,4},{6,7},{7,6},{8,9},{9,8},{10,11... | collective-permute-start | bytes 3538952 | tf_op jit(solution)/shard_map/ppermute | solution.py:171
  2.9 28.1 %copy-start.9 = (f32[128]{0:T(128)S(1)}, f32[128]{0:T(128)}, u32[]{:S(2)}) copy-start(f32[128]{0:T(128)} %param.10) | copy-start | bytes 1540
  37.5 22.6 %collective-permute-start.1 = (bf16[2,384,512]{2,1,0:T(8,128)(2,1)}, bf16[2,384,512]{2,1,0:T(8,128)(2,1)S(1)}, u32[]{:S(2)}, u32[]{:S(2)}) collective-permute-start(bf16[2,384,512]{2,1,0:T(8,128)(2,1)} %project.5.refs_0_), channel_id=1, source_target_pairs={{0,8},{2,10},{4,12},{6,14},{8,16},{10,18},{12,20},{14,22},{16,24},... | collective-permute-start | bytes 2359304 | tf_op jit(solution)/shard_map/ppermute | solution.py:171
  39.4 36.5 %collective-permute-start.2 = (bf16[2,384,512]{2,1,0:T(8,128)(2,1)}, bf16[2,384,512]{2,1,0:T(8,128)(2,1)}, u32[]{:S(2)}, u32[]{:S(2)}) collective-permute-start(bf16[2,384,512]{2,1,0:T(8,128)(2,1)} %project.5.refs_0_), channel_id=1, source_target_pairs={{0,24},{2,26},{4,28},{6,30},{8,0},{10,2},{12,4},{14,6},{16,8},{18,... | collective-permute-start | bytes 2359304 | tf_op jit(solution)/shard_map/ppermute | solution.py:171
  41.4 37.5 %collective-permute-start.3 = (bf16[2,384,512]{2,1,0:T(8,128)(2,1)}, bf16[2,384,512]{2,1,0:T(8,128)(2,1)}, u32[]{:S(2)}, u32[]{:S(2)}) collective-permute-start(bf16[2,384,512]{2,1,0:T(8,128)(2,1)} %project.5.refs_0_), channel_id=1, source_target_pairs={{0,4},{2,6},{4,0},{6,2},{8,12},{10,14},{12,8},{14,10},{16,20},{18,... | collective-permute-start | bytes 2359304 | tf_op jit(solution)/shard_map/ppermute | solution.py:171
  43.1 37.3 %collective-permute-start.5 = (bf16[2,384,512]{2,1,0:T(8,128)(2,1)}, bf16[2,384,512]{2,1,0:T(8,128)(2,1)}, u32[]{:S(2)}, u32[]{:S(2)}) collective-permute-start(bf16[2,384,512]{2,1,0:T(8,128)(2,1)} %project.5.refs_0_), channel_id=1, source_target_pairs={{0,2},{2,0},{4,6},{6,4},{8,10},{10,8},{12,14},{14,12},{16,18},{18,... | collective-permute-start | bytes 2359304 | tf_op jit(solution)/shard_map/ppermute | solution.py:171
  46.4 103.4 %collective-permute-start.28 = (bf16[768,1536]{1,0:T(8,128)(2,1)}, bf16[768,1536]{1,0:T(8,128)(2,1)}, u32[]{:S(2)}, u32[]{:S(2)}) collective-permute-start(bf16[768,1536]{1,0:T(8,128)(2,1)} %dynamic_slice.12), channel_id=1, source_target_pairs={{0,1},{1,0},{2,3},{3,2},{4,5},{5,4},{6,7},{7,6},{8,9},{9,8},{10,11... | collective-permute-start | bytes 7077896 | tf_op jit(solution)/shard_map/ppermute | solution.py:171
  60.1 34.7 %collective-permute-start.9 = (bf16[2,384,512]{2,1,0:T(8,128)(2,1)}, bf16[2,384,512]{2,1,0:T(8,128)(2,1)}, u32[]{:S(2)}, u32[]{:S(2)}) collective-permute-start(bf16[2,384,512]{2,1,0:T(8,128)(2,1)} %project.6.refs_0_), channel_id=1, source_target_pairs={{0,8},{2,10},{4,12},{6,14},{8,16},{10,18},{12,20},{14,22},{16,24},... | collective-permute-start | bytes 2359304 | tf_op jit(solution)/shard_map/ppermute | solution.py:171
  75.8 35.7 %collective-permute-start.10 = (bf16[2,384,512]{2,1,0:T(8,128)(2,1)}, bf16[2,384,512]{2,1,0:T(8,128)(2,1)}, u32[]{:S(2)}, u32[]{:S(2)}) collective-permute-start(bf16[2,384,512]{2,1,0:T(8,128)(2,1)} %project.6.refs_0_), channel_id=1, source_target_pairs={{0,24},{2,26},{4,28},{6,30},{8,0},{10,2},{12,4},{14,6},{16,8},{18,... | collective-permute-start | bytes 2359304 | tf_op jit(solution)/shard_map/ppermute | solution.py:171
  78.9 33.7 %collective-permute-start.11 = (bf16[2,384,512]{2,1,0:T(8,128)(2,1)}, bf16[2,384,512]{2,1,0:T(8,128)(2,1)}, u32[]{:S(2)}, u32[]{:S(2)}) collective-permute-start(bf16[2,384,512]{2,1,0:T(8,128)(2,1)} %project.6.refs_0_), channel_id=1, source_target_pairs={{0,4},{2,6},{4,0},{6,2},{8,12},{10,14},{12,8},{14,10},{16,20},{18,... | collective-permute-start | bytes 2359304 | tf_op jit(solution)/shard_map/ppermute | solution.py:171
  80.4 33.7 %collective-permute-start.13 = (bf16[2,384,512]{2,1,0:T(8,128)(2,1)}, bf16[2,384,512]{2,1,0:T(8,128)(2,1)}, u32[]{:S(2)}, u32[]{:S(2)}) collective-permute-start(bf16[2,384,512]{2,1,0:T(8,128)(2,1)} %project.6.refs_0_), channel_id=1, source_target_pairs={{0,2},{2,0},{4,6},{6,4},{8,10},{10,8},{12,14},{14,12},{16,18},{18,... | collective-permute-start | bytes 2359304 | tf_op jit(solution)/shard_map/ppermute | solution.py:171
  86.2 30.0 %copy-start.7 = (bf16[2,384,512]{2,1,0:T(8,128)(2,1)}, bf16[2,384,512]{2,1,0:T(8,128)(2,1)S(1)}, u32[]{:S(2)}) copy-start(bf16[2,384,512]{2,1,0:T(8,128)(2,1)S(1)} %project.7.refs_0_) | copy-start | bytes 2359300
  94.8 34.7 %collective-permute-start.17 = (bf16[2,384,512]{2,1,0:T(8,128)(2,1)S(1)}, bf16[2,384,512]{2,1,0:T(8,128)(2,1)S(1)}, u32[]{:S(2)}, u32[]{:S(2)}) collective-permute-start(bf16[2,384,512]{2,1,0:T(8,128)(2,1)S(1)} %project.7.refs_0_), channel_id=1, source_target_pairs={{0,8},{2,10},{4,12},{6,14},{8,16},{10,18},{12,20},{14,22},{16,24},... | collective-permute-start | bytes 2359304 | tf_op jit(solution)/shard_map/ppermute | solution.py:171
  111.5 31.1 %collective-permute-start.18 = (bf16[2,384,512]{2,1,0:T(8,128)(2,1)S(1)}, bf16[2,384,512]{2,1,0:T(8,128)(2,1)S(1)}, u32[]{:S(2)}, u32[]{:S(2)}) collective-permute-start(bf16[2,384,512]{2,1,0:T(8,128)(2,1)S(1)} %project.7.refs_0_), channel_id=1, source_target_pairs={{0,24},{2,26},{4,28},{6,30},{8,0},{10,2},{12,4},{14,6},{16,8},{18,... | collective-permute-start | bytes 2359304 | tf_op jit(solution)/shard_map/ppermute | solution.py:171
  112.6 30.1 %collective-permute-start.19 = (bf16[2,384,512]{2,1,0:T(8,128)(2,1)S(1)}, bf16[2,384,512]{2,1,0:T(8,128)(2,1)S(1)}, u32[]{:S(2)}, u32[]{:S(2)}) collective-permute-start(bf16[2,384,512]{2,1,0:T(8,128)(2,1)S(1)} %project.7.refs_0_), channel_id=1, source_target_pairs={{0,4},{2,6},{4,0},{6,2},{8,12},{10,14},{12,8},{14,10},{16,20},{18,... | collective-permute-start | bytes 2359304 | tf_op jit(solution)/shard_map/ppermute | solution.py:171
  114.1 35.7 %collective-permute-start.4 = (bf16[2,384,512]{2,1,0:T(8,128)(2,1)S(1)}, bf16[2,384,512]{2,1,0:T(8,128)(2,1)}, u32[]{:S(2)}, u32[]{:S(2)}) collective-permute-start(bf16[2,384,512]{2,1,0:T(8,128)(2,1)S(1)} %get-tuple-element.16), channel_id=1, source_target_pairs={{0,4},{2,6},{4,0},{6,2},{8,12},{10,14},{12,8},{14,10},{16,20},{18,... | collective-permute-start | bytes 2359304 | tf_op jit(solution)/shard_map/ppermute | solution.py:171
  116.1 52.2 %copy-start.20 = (s32[16]{0:T(128)S(1)}, s32[16]{0:T(128)}, u32[]{:S(2)}) copy-start(s32[16]{0:T(128)} %param.13) | copy-start | bytes 196
  116.1 66.0 %copy-start.10 = (f32[128]{0:T(128)S(1)}, f32[128]{0:T(128)}, u32[]{:S(2)}) copy-start(f32[128]{0:T(128)} %param.9) | copy-start | bytes 1540
  129.5 23.0 %collective-permute-start.6 = (bf16[2,384,512]{2,1,0:T(8,128)(2,1)S(1)}, bf16[2,384,512]{2,1,0:T(8,128)(2,1)S(1)}, u32[]{:S(2)}, u32[]{:S(2)}) collective-permute-start(bf16[2,384,512]{2,1,0:T(8,128)(2,1)S(1)} %get-tuple-element.15), channel_id=1, source_target_pairs={{0,2},{2,0},{4,6},{6,4},{8,10},{10,8},{12,14},{14,12},{16,18},{18,... | collective-permute-start | bytes 2359304 | tf_op jit(solution)/shard_map/ppermute | solution.py:171
  142.6 9.0 %copy-start.5 = (bf16[2,384,512]{2,1,0:T(8,128)(2,1)}, bf16[2,384,512]{2,1,0:T(8,128)(2,1)S(1)}, u32[]{:S(2)}) copy-start(bf16[2,384,512]{2,1,0:T(8,128)(2,1)S(1)} %collective-permute-done.18.refs_2_) | copy-start | bytes 2359300
  142.6 10.8 %collective-permute-start.7 = (bf16[2,384,512]{2,1,0:T(8,128)(2,1)}, bf16[2,384,512]{2,1,0:T(8,128)(2,1)S(1)}, u32[]{:S(2)}, u32[]{:S(2)}) collective-permute-start(bf16[2,384,512]{2,1,0:T(8,128)(2,1)} %collective-permute-done.3.refs_3_), channel_id=1, source_target_pairs={{0,2},{2,0},{4,6},{6,4},{8,10},{10,8},{12,14},{14,12},{16,18},{18,... | collective-permute-start | bytes 2359304 | tf_op jit(solution)/shard_map/ppermute | solution.py:171
  142.7 9.8 %copy-start.11 = (bf16[2,384,512]{2,1,0:T(8,128)(2,1)}, bf16[2,384,512]{2,1,0:T(8,128)(2,1)S(1)}, u32[]{:S(2)}) copy-start(bf16[2,384,512]{2,1,0:T(8,128)(2,1)S(1)} %collective-permute-done.19.refs_3_) | copy-start | bytes 2359300
  142.7 23.9 %collective-permute-start.12 = (bf16[2,384,512]{2,1,0:T(8,128)(2,1)S(1)}, bf16[2,384,512]{2,1,0:T(8,128)(2,1)}, u32[]{:S(2)}, u32[]{:S(2)}) collective-permute-start(bf16[2,384,512]{2,1,0:T(8,128)(2,1)S(1)} %get-tuple-element.14), channel_id=1, source_target_pairs={{0,4},{2,6},{4,0},{6,2},{8,12},{10,14},{12,8},{14,10},{16,20},{18,... | collective-permute-start | bytes 2359304 | tf_op jit(solution)/shard_map/ppermute | solution.py:171
  149.8 16.9 %collective-permute-start.14 = (bf16[2,384,512]{2,1,0:T(8,128)(2,1)S(1)}, bf16[2,384,512]{2,1,0:T(8,128)(2,1)S(1)}, u32[]{:S(2)}, u32[]{:S(2)}) collective-permute-start(bf16[2,384,512]{2,1,0:T(8,128)(2,1)S(1)} %get-tuple-element.13), channel_id=1, source_target_pairs={{0,2},{2,0},{4,6},{6,4},{8,10},{10,8},{12,14},{14,12},{16,18},{18,... | collective-permute-start | bytes 2359304 | tf_op jit(solution)/shard_map/ppermute | solution.py:171
  149.8 96.7 %collective-permute-start.29 = (bf16[768,1536]{1,0:T(8,128)(2,1)}, bf16[768,1536]{1,0:T(8,128)(2,1)}, u32[]{:S(2)}, u32[]{:S(2)}) collective-permute-start(bf16[768,1536]{1,0:T(8,128)(2,1)} %collective-permute-done.28), channel_id=1, source_target_pairs={{0,2},{2,0},{4,6},{6,4},{8,10},{10,8},{12,14},{14,12},{16,18},{18,... | collective-permute-start | bytes 7077896 | tf_op jit(solution)/shard_map/ppermute | solution.py:171
  151.6 0.9 copy-start.3
  152.5 0.9 copy-start.13
  153.4 16.2 %collective-permute-start.15 = (bf16[2,384,512]{2,1,0:T(8,128)(2,1)}, bf16[2,384,512]{2,1,0:T(8,128)(2,1)}, u32[]{:S(2)}, u32[]{:S(2)}) collective-permute-start(bf16[2,384,512]{2,1,0:T(8,128)(2,1)} %collective-permute-done.11.refs_3_), channel_id=1, source_target_pairs={{0,2},{2,0},{4,6},{6,4},{8,10},{10,8},{12,14},{14,12},{16,18},{18,... | collective-permute-start | bytes 2359304 | tf_op jit(solution)/shard_map/ppermute | solution.py:171
  153.4 13.3 %copy-start.17 = (bf16[2,384,512]{2,1,0:T(8,128)(2,1)}, bf16[2,384,512]{2,1,0:T(8,128)(2,1)S(1)}, u32[]{:S(2)}) copy-start(bf16[2,384,512]{2,1,0:T(8,128)(2,1)S(1)} %collective-permute-done.7.refs_7_) | copy-start | bytes 2359300
  153.4 28.1 %collective-permute-start.20 = (bf16[2,384,512]{2,1,0:T(8,128)(2,1)}, bf16[2,384,512]{2,1,0:T(8,128)(2,1)}, u32[]{:S(2)}, u32[]{:S(2)}) collective-permute-start(bf16[2,384,512]{2,1,0:T(8,128)(2,1)} %get-tuple-element.12), channel_id=1, source_target_pairs={{0,4},{2,6},{4,0},{6,2},{8,12},{10,14},{12,8},{14,10},{16,20},{18,... | collective-permute-start | bytes 2359304 | tf_op jit(solution)/shard_map/ppermute | solution.py:171
  166.7 14.9 %collective-permute-start.8 = (bf16[2,384,512]{2,1,0:T(8,128)(2,1)}, bf16[2,384,512]{2,1,0:T(8,128)(2,1)}, u32[]{:S(2)}, u32[]{:S(2)}) collective-permute-start(bf16[2,384,512]{2,1,0:T(8,128)(2,1)} %collective-permute-done.4.refs_4_), channel_id=1, source_target_pairs={{0,2},{2,0},{4,6},{6,4},{8,10},{10,8},{12,14},{14,12},{16,18},{18,... | collective-permute-start | bytes 2359304 | tf_op jit(solution)/shard_map/ppermute | solution.py:171
  166.7 0.9 copy-start.15
  167.6 14.5 %collective-permute-start.16 = (bf16[2,384,512]{2,1,0:T(8,128)(2,1)}, bf16[2,384,512]{2,1,0:T(8,128)(2,1)}, u32[]{:S(2)}, u32[]{:S(2)}) collective-permute-start(bf16[2,384,512]{2,1,0:T(8,128)(2,1)} %collective-permute-done.12.refs_4_), channel_id=1, source_target_pairs={{0,2},{2,0},{4,6},{6,4},{8,10},{10,8},{12,14},{14,12},{16,18},{18,... | collective-permute-start | bytes 2359304 | tf_op jit(solution)/shard_map/ppermute | solution.py:171
  169.7 54.8 %collective-permute-start.21 = (bf16[2,384,512]{2,1,0:T(8,128)(2,1)}, bf16[2,384,512]{2,1,0:T(8,128)(2,1)S(1)}, u32[]{:S(2)}, u32[]{:S(2)}) collective-permute-start(bf16[2,384,512]{2,1,0:T(8,128)(2,1)} %copy-done.7), channel_id=1, source_target_pairs={{0,2},{2,0},{4,6},{6,4},{8,10},{10,8},{12,14},{14,12},{16,18},{18,... | collective-permute-start | bytes 2359304 | tf_op jit(solution)/shard_map/ppermute | solution.py:171
  181.6 44.5 %collective-permute-start.22 = (bf16[2,384,512]{2,1,0:T(8,128)(2,1)}, bf16[2,384,512]{2,1,0:T(8,128)(2,1)S(1)}, u32[]{:S(2)}, u32[]{:S(2)}) collective-permute-start(bf16[2,384,512]{2,1,0:T(8,128)(2,1)} %get-tuple-element.11), channel_id=1, source_target_pairs={{0,2},{2,0},{4,6},{6,4},{8,10},{10,8},{12,14},{14,12},{16,18},{18,... | collective-permute-start | bytes 2359304 | tf_op jit(solution)/shard_map/ppermute | solution.py:171
  181.6 45.0 %collective-permute-start.23 = (bf16[2,384,512]{2,1,0:T(8,128)(2,1)}, bf16[2,384,512]{2,1,0:T(8,128)(2,1)S(1)}, u32[]{:S(2)}, u32[]{:S(2)}) collective-permute-start(bf16[2,384,512]{2,1,0:T(8,128)(2,1)} %copy-done.11), channel_id=1, source_target_pairs={{0,2},{2,0},{4,6},{6,4},{8,10},{10,8},{12,14},{14,12},{16,18},{18,... | collective-permute-start | bytes 2359304 | tf_op jit(solution)/shard_map/ppermute | solution.py:171
  182.1 44.5 %collective-permute-start.24 = (bf16[2,384,512]{2,1,0:T(8,128)(2,1)}, bf16[2,384,512]{2,1,0:T(8,128)(2,1)S(1)}, u32[]{:S(2)}, u32[]{:S(2)}) collective-permute-start(bf16[2,384,512]{2,1,0:T(8,128)(2,1)} %collective-permute-done.20.refs_4_), channel_id=1, source_target_pairs={{0,2},{2,0},{4,6},{6,4},{8,10},{10,8},{12,14},{14,12},{16,18},{18,... | collective-permute-start | bytes 2359304 | tf_op jit(solution)/shard_map/ppermute | solution.py:171
  182.2 9.2 %copy-start.14 = (bf16[2,384,512]{2,1,0:T(8,128)(2,1)S(1)}, bf16[2,384,512]{2,1,0:T(8,128)(2,1)}, u32[]{:S(2)}) copy-start(bf16[2,384,512]{2,1,0:T(8,128)(2,1)} %copy-done.13) | copy-start | bytes 2359300
  190.3 1.0 copy-start.2
  191.4 16.4 %copy-start.16 = (bf16[2,384,512]{2,1,0:T(8,128)(2,1)S(1)}, bf16[2,384,512]{2,1,0:T(8,128)(2,1)}, u32[]{:S(2)}) copy-start(bf16[2,384,512]{2,1,0:T(8,128)(2,1)} %copy-done.15) | copy-start | bytes 2359300
  207.7 20.8 %copy-start.4 = (bf16[2,384,512]{2,1,0:T(8,128)(2,1)S(1)}, bf16[2,384,512]{2,1,0:T(8,128)(2,1)}, u32[]{:S(2)}) copy-start(bf16[2,384,512]{2,1,0:T(8,128)(2,1)} %copy-done.3) | copy-start | bytes 2359300
  207.8 20.8 %copy-start.6 = (bf16[2,384,512]{2,1,0:T(8,128)(2,1)S(1)}, bf16[2,384,512]{2,1,0:T(8,128)(2,1)}, u32[]{:S(2)}) copy-start(bf16[2,384,512]{2,1,0:T(8,128)(2,1)} %copy-done.5) | copy-start | bytes 2359300
  207.8 20.8 %copy-start.8 = (bf16[2,384,512]{2,1,0:T(8,128)(2,1)S(1)}, bf16[2,384,512]{2,1,0:T(8,128)(2,1)}, u32[]{:S(2)}) copy-start(bf16[2,384,512]{2,1,0:T(8,128)(2,1)} %copy-done.7) | copy-start | bytes 2359300
  207.8 20.8 %copy-start.12 = (bf16[2,384,512]{2,1,0:T(8,128)(2,1)S(1)}, bf16[2,384,512]{2,1,0:T(8,128)(2,1)}, u32[]{:S(2)}) copy-start(bf16[2,384,512]{2,1,0:T(8,128)(2,1)} %copy-done.11) | copy-start | bytes 2359300
  224.5 26.2 %collective-permute-start.25 = (bf16[384,512]{1,0:T(8,128)(2,1)S(1)}, bf16[384,512]{1,0:T(8,128)(2,1)S(1)}, u32[]{:S(2)}, u32[]{:S(2)}) collective-permute-start(bf16[384,512]{1,0:T(8,128)(2,1)S(1)} %attend.3.refs_0_), channel_id=1, source_target_pairs={{0,1},{1,0},{2,3},{3,2},{4,5},{5,4},{6,7},{7,6},{8,9},{9,8},{10,11... | collective-permute-start | bytes 1179656 | tf_op jit(solution)/shard_map/ppermute | solution.py:171
  226.0 24.6 %collective-permute-start.26 = (bf16[384,512]{1,0:T(8,128)(2,1)S(1)}, bf16[384,512]{1,0:T(8,128)(2,1)S(1)}, u32[]{:S(2)}, u32[]{:S(2)}) collective-permute-start(bf16[384,512]{1,0:T(8,128)(2,1)S(1)} %attend.4.refs_1_), channel_id=1, source_target_pairs={{0,1},{1,0},{2,3},{3,2},{4,5},{5,4},{6,7},{7,6},{8,9},{9,8},{10,11... | collective-permute-start | bytes 1179656 | tf_op jit(solution)/shard_map/ppermute | solution.py:171
  226.6 0.9 copy-start.18
  227.5 1.0 copy-start.19
  245.0 7.8 %collective-permute-start.27 = (bf16[384,512]{1,0:T(8,128)(2,1)S(1)}, bf16[384,512]{1,0:T(8,128)(2,1)S(1)}, u32[]{:S(2)}, u32[]{:S(2)}) collective-permute-start(bf16[384,512]{1,0:T(8,128)(2,1)S(1)} %attend.5.refs_2_), channel_id=1, source_target_pairs={{0,1},{1,0},{2,3},{3,2},{4,5},{5,4},{6,7},{7,6},{8,9},{9,8},{10,11... | collective-permute-start | bytes 1179656 | tf_op jit(solution)/shard_map/ppermute | solution.py:171
  252.8 8.0 %copy-start.1 = (s32[16,6]{0,1:T(8,128)S(1)}, s32[16,6]{0,1:T(8,128)}, u32[]{:S(2)}) copy-start(s32[16,6]{0,1:T(8,128)} %param.12) | copy-start | bytes 1156

commit v2 on v1

v2 whole, which is shorter than its diff:
```python
import functools

import jax
import jax.numpy as jnp
from jax import lax
from jax.experimental import pallas as pl
from jax.experimental.pallas import tpu as pltpu
from jax.sharding import PartitionSpec as P

HD = 128
TILE = 384
EPS = 1e-06
LOG2E = 1.4426950408889634
VMEM = 48 * 1024 * 1024


def width_of(columns):
    return 256 if columns % 256 == 0 else 128


def normed(product, gain):
    parts = []
    for first in range(0, product.shape[1], HD):
        head = product[:, first : first + HD]
        factor = lax.rsqrt(jnp.mean(head * head, axis=-1, keepdims=True) + EPS)
        parts.append(head * factor * gain)
    return parts[0] if len(parts) == 1 else jnp.concatenate(parts, axis=1)


def project_kernel(low_ref, high_ref, w_ref, gain_ref, out_ref):
    half = low_ref.shape[1]
    product = jnp.dot(low_ref[...], w_ref[0, :half, :], preferred_element_type=jnp.float32)
    product += jnp.dot(high_ref[...], w_ref[0, half:, :], preferred_element_type=jnp.float32)

    @pl.when(pl.program_id(0) == 0)
    def _():
        out_ref[0] = normed(product, gain_ref[...]).astype(out_ref.dtype)

    @pl.when(pl.program_id(0) != 0)
    def _():
        out_ref[0] = product.astype(out_ref.dtype)


def project(low, high, w, gain, kind, kinds, first_col, columns):
    rows, half = low.shape
    depth = w.shape[1]
    wide = width_of(columns)
    base = first_col // wide
    return pl.pallas_call(
        project_kernel,
        grid=(kinds, columns // wide),
        in_specs=[
            pl.BlockSpec((rows, half), lambda i, j: (0, 0)),
            pl.BlockSpec((rows, half), lambda i, j: (0, 0)),
            pl.BlockSpec((1, depth, wide), lambda i, j: (kind + i, 0, base + j)),
            pl.BlockSpec((1, HD), lambda i, j: (0, 0)),
        ],
        out_specs=pl.BlockSpec((1, rows, wide), lambda i, j: (i, 0, j)),
        out_shape=jax.ShapeDtypeStruct((kinds, rows, columns), jnp.bfloat16),
        compiler_params=pltpu.CompilerParams(vmem_limit_bytes=VMEM),
        cost_estimate=pl.CostEstimate(
            flops=2 * rows * depth * columns * kinds,
            bytes_accessed=2 * depth * columns * kinds + 2 * rows * (depth + columns * kinds),
            transcendentals=0,
        ),
        name="project",
    )(low, high, w, gain)


def attend_kernel(pieces, used_ref, q_ref, *refs):
    blocks = [refs[first : first + pieces] for first in range(0, 9 * pieces, pieces)]
    out_ref, top, total, acc = refs[9 * pieces :]
    top[...] = jnp.full(top.shape, -jnp.inf, jnp.float32)
    total[...] = jnp.zeros(total.shape, jnp.float32)
    acc[...] = jnp.zeros(acc.shape, jnp.float32)
    scale = HD ** (-0.5) * LOG2E
    heads = q_ref.shape[2] // HD
    for index, block in enumerate(blocks):

        @pl.when(used_ref[index] != 0)
        def _(block=block):
            for piece in block:
                for head in range(heads):
                    cols = slice(head * HD, (head + 1) * HD)
                    scores = lax.dot_general(
                        piece[0, :, cols],
                        q_ref[0, :, cols],
                        (((1,), (1,)), ((), ())),
                        preferred_element_type=jnp.float32,
                    ) * scale
                    before = top[head]
                    now = jnp.maximum(before, jnp.max(scores, axis=0, keepdims=True))
                    shrink = jnp.exp2(before - now)
                    expo = jnp.exp2(scores - now)
                    top[head] = now
                    total[head] = total[head] * shrink + jnp.sum(expo, axis=0, keepdims=True)
                    acc[head] = acc[head] * shrink + lax.dot_general(
                        piece[1, :, cols],
                        expo.astype(jnp.bfloat16),
                        (((0,), (0,)), ((), ())),
                        preferred_element_type=jnp.float32,
                    )

    for head in range(heads):
        cols = slice(head * HD, (head + 1) * HD)
        out_ref[:, cols] = (acc[head] / total[head]).T.astype(out_ref.dtype)


def attend(used, queries, blocks, first_col, columns):
    rows = queries.shape[1]
    wide = width_of(columns)
    base = first_col // wide
    heads = wide // HD
    pieces = len(blocks[0])
    flat = [piece for block in blocks for piece in block]
    specs = [pl.BlockSpec((2, piece.shape[1], wide), lambda h, used: (0, 0, h)) for piece in flat]
    return pl.pallas_call(
        functools.partial(attend_kernel, pieces),
        grid_spec=pltpu.PrefetchScalarGridSpec(
            num_scalar_prefetch=1,
            grid=(columns // wide,),
            in_specs=[pl.BlockSpec((1, rows, wide), lambda h, used: (0, 0, base + h))] + specs,
            out_specs=pl.BlockSpec((rows, wide), lambda h, used: (0, h)),
            scratch_shapes=[
                pltpu.VMEM((heads, 1, rows), jnp.float32),
                pltpu.VMEM((heads, 1, rows), jnp.float32),
                pltpu.VMEM((heads, HD, rows), jnp.float32),
            ],
        ),
        out_shape=jax.ShapeDtypeStruct((rows, columns), jnp.bfloat16),
        compiler_params=pltpu.CompilerParams(vmem_limit_bytes=VMEM),
        cost_estimate=pl.CostEstimate(
            flops=24 * rows * rows * 9 * columns,
            bytes_accessed=2 * rows * columns * 20,
            transcendentals=9 * rows * rows * (columns // HD),
        ),
        name="attend",
    )(used, queries, *flat)


def mix_kernel(first, side_ref, own_ref, other_ref, w_own, w_other, *refs):
    out_ref = refs[-1]
    product = jnp.dot(own_ref[...], w_own[...], preferred_element_type=jnp.float32)
    product += jnp.dot(other_ref[...], w_other[...], preferred_element_type=jnp.float32)
    if not first:
        product += refs[0][...]
    out_ref[...] = product.astype(out_ref.dtype)


def mix(side, own, other, w_out, w_other, first_col, so_far, kind):
    rows, columns = own.shape
    width = w_other.shape[1]
    wide = width_of(width)
    steps = width // wide
    base = first_col // columns
    piece = pl.BlockSpec((rows, columns), lambda j, side: (0, 0))
    strip = pl.BlockSpec((rows, wide), lambda j, side: (0, j))
    more = [] if so_far is None else [so_far]
    return pl.pallas_call(
        functools.partial(mix_kernel, so_far is None),
        grid_spec=pltpu.PrefetchScalarGridSpec(
            num_scalar_prefetch=1,
            grid=(steps,),
            in_specs=[
                piece,
                piece,
                pl.BlockSpec((columns, wide), lambda j, side: (base, side[0] * steps + j)),
                pl.BlockSpec((columns, wide), lambda j, side: (base, j)),
            ]
            + [strip] * len(more),
            out_specs=strip,
        ),
        out_shape=jax.ShapeDtypeStruct((rows, width), kind),
        compiler_params=pltpu.CompilerParams(vmem_limit_bytes=VMEM),
        cost_estimate=pl.CostEstimate(
            flops=4 * rows * columns * width, bytes_accessed=4 * columns * width, transcendentals=0
        ),
        name="mix",
    )(side, own, other, w_out, w_other, *more)


def after(value, *others):
    return lax.optimization_barrier((value,) + others)[0]


def shifted(value, axis, target):
    count = lax.axis_size(axis)
    return lax.ppermute(value, axis, [(s, target(s) % count) for s in range(count)])


def on_device(tokens, w_qkv, q_gain, k_gain, w_out, neighbours, counts):
    columns = w_qkv.shape[2]
    heads_here = columns // HD
    total_tiles = neighbours.shape[0]
    sides = lax.axis_size("mp")
    side = lax.axis_index("mp")
    tile = lax.axis_index("seq")
    core, row = tile % 2, (tile // 2) % 2
    splits = (4, 4, 2, 2) if heads_here == 12 else (1,) * heads_here
    widths = [heads * HD for heads in splits]
    starts = [sum(widths[:part]) for part in range(len(widths))]

    w = jnp.transpose(w_qkv, (1, 0, 2))
    q_gain, k_gain = q_gain.reshape(1, HD), k_gain.reshape(1, HD)

    if sides == 2:
        mine = jnp.split(tokens, 2, axis=0)
        across = [shifted(half, "mp", lambda s: s + 1) for half in mine]
        lows = [jnp.where(side == 0, here, there) for here, there in zip(mine, across)]
        highs = [jnp.where(side == 0, there, here) for here, there in zip(mine, across)]
    else:
        across = [lax.all_gather(tokens, "mp", axis=1, tiled=True)]
        low, high = jnp.split(across[0], 2, axis=1)
        lows, highs = [low], [high]

    turn = jnp.where(row == 0, -4, 4)
    spin = jnp.where(core == 0, -4, 4)
    held = jnp.stack(
        [tile, tile - 4, tile + 4, tile ^ 2, (tile ^ 2) + turn,
         tile ^ 1, (tile ^ 1) + spin, tile ^ 3, (tile ^ 3) + turn]
    )
    held = jnp.mod(held, total_tiles)
    listed = lax.dynamic_index_in_dim(neighbours, tile, 0, keepdims=False)
    in_use = jnp.arange(listed.shape[0], dtype=jnp.int32) < counts[tile]
    used = jnp.any((held[:, None] == listed[None, :]) & in_use[None, :], axis=1).astype(jnp.int32)

    low = high = queries = None
    windows, attended = [], []
    past_beyond = None
    for part in range(len(widths)):
        start, width = starts[part], widths[part]
        if part == 0:
            owns = [project(a, b, w, k_gain, 1, 2, start, width) for a, b in zip(lows, highs)]
        else:
            if part == 1:
                low, high = jnp.concatenate(lows, axis=0), jnp.concatenate(highs, axis=0)
            if part == 2:
                low, high, _ = lax.optimization_barrier((low, high, queries))
            owns = [project(low, high, w, k_gain, 1, 2, start, width)]
        pieces = []
        for own in owns:
            below = shifted(own, "seq", lambda s: s + 4)
            above = shifted(own, "seq", lambda s: s - 4)
            held_up = own if past_beyond is None else after(own, past_beyond)
            beside = shifted(held_up, "seq", lambda s: s ^ 2)
            twin = shifted(own, "seq", lambda s: s ^ 1)
            onward = jnp.where(row == 1, below, above)
            if part >= 2:
                onward = after(onward, attended[part - 2])
            beyond = shifted(onward, "seq", lambda s: s ^ 2)
            past_beyond = beyond
            twin_far = shifted(jnp.where(core == 1, below, above), "seq", lambda s: s ^ 1)
            twin_beside = shifted(beside, "seq", lambda s: s ^ 1)
            handed = beyond if part < 2 else after(beyond, attended[part - 1])
            twin_beyond = shifted(handed, "seq", lambda s: s ^ 1)
            pieces.append(
                [own, below, above, beside, beyond, twin, twin_far, twin_beside, twin_beyond]
            )
        window = [list(block) for block in zip(*pieces)]
        windows.append(window)
        if part == 1:
            queries = project(low, high, w, q_gain, 0, 1, 0, columns)
        if part >= 1:
            for done in range(len(attended), part + 1):
                attended.append(attend(used, queries, windows[done], starts[done], widths[done]))

    if sides == 2:
        depth, width = w_out.shape[0] // 2, w_out.shape[1] // 2
        sent = lax.dynamic_slice(w_out, (core * depth, (1 - side) * width), (depth, width))
        sent = after(sent, *across)
        got = shifted(sent, "mp", lambda s: s + 1)
        got_twin = shifted(got, "seq", lambda s: s ^ 1)
        w_other = jnp.concatenate(
            [jnp.where(core == 0, got, got_twin), jnp.where(core == 0, got_twin, got)], axis=0
        )
        flag = side.reshape(1).astype(jnp.int32)
        total = None
        for part, piece in enumerate(attended):
            other = shifted(piece, "mp", lambda s: s + 1)
            kind = jnp.bfloat16 if part == len(attended) - 1 else jnp.float32
            total = mix(flag, piece, other, w_out, w_other, starts[part], total, kind)
        return total
    terms = jnp.dot(
        jnp.concatenate(attended, axis=1), w_out, preferred_element_type=jnp.float32
    ).astype(jnp.bfloat16)
    return lax.psum_scatter(terms, "mp", scatter_dimension=1, tiled=True)


def solution(mesh):
    return jax.shard_map(
        on_device,
        mesh=mesh,
        in_specs=(P("seq", "mp"), P(None, None, "mp"), P(), P(), P("mp", None), P(), P()),
        out_specs=P("seq", "mp"),
        check_vma=False,
    )
```

time: 262 us -> 263 us (level); the launches traced: 261 us -> 258 us
  Pallas kernels: 84.4 us -> 96.6 us
  starting transfers between devices: 51.1 us -> 40.9 us
  waiting for transfers between devices: 105 us -> 98.1 us
  other arithmetic: 10.5 us -> 15.3 us
  local copies, waits for them, and re-layouts: 9.83 us -> 6.57 us
    ppermute x30 -> x48, starting transfers between devices: 51.1 us -> 40.9 us  [shifted(): lax.ppermute(value, axis, [(s, target(s) % count) for s in range(count)])]
    pallas_call x4 -> x8, Pallas kernels: 57.4 us -> 65 us  [the longest x4 45.9 us: attend(): pl.pallas_call(functools.partial(attend_kernel, pieces), grid_spec=pltpu....]
    ppermute x30 -> x48, waiting for transfers between devices: 105 us -> 98.1 us  [shifted(): lax.ppermute(value, axis, [(s, target(s) % count) for s in range(count)])]
    pallas_call x4 -> x6, Pallas kernels: 27 us -> 31.6 us  [project(): pl.pallas_call(project_kernel, grid=(kinds, columns // wide), in_specs=[p...]
    unnamed x42 -> x44, local copies, waits for them, and re-layouts: 5.71 us -> 2.66 us
    select_n x3 -> x5, other arithmetic: 3.96 us -> 6.31 us  [on_device(): jnp.where(core == 1, below, above)]
    select_n x2 -> x3, other arithmetic: 5.88 us -> 5.59 us  [the longest x2 3.32 us: on_device(): jnp.where(side == 0, there, here)]
  transfers between devices with their start and end apart: 30 -> 48, of which waited for: 11 -> 9; matrix products, arithmetic and copies ran while one was open for 5% -> 6% of each run, Pallas kernels for 27% -> 33%
where the time goes in v2:
time: 263 us; the launch traced here: 258 us
  waiting for transfers between devices  98.1 us (37%)
  Pallas kernels  96.6 us (37%)
  starting transfers between devices  40.9 us (16%)
  other arithmetic  15.3 us (6%)
  local copies, waits for them, and re-layouts  6.57 us (2%)
    ppermute x48, waiting for transfers between devices, shifted(): lax.ppermute(value, axis, [(s, target(s) % count) for s in range(count)])  98.1 us
    pallas_call x4, Pallas kernels, attend(): pl.pallas_call(functools.partial(attend_kernel, pieces), grid_spec=pltpu....  45.9 us
    ppermute x48, starting transfers between devices, shifted(): lax.ppermute(value, axis, [(s, target(s) % count) for s in range(count)])  40.9 us
    pallas_call x6, Pallas kernels, project(): pl.pallas_call(project_kernel, grid=(kinds, columns // wide), in_specs=[p...  31.6 us
    pallas_call x4, Pallas kernels, mix(): pl.pallas_call(functools.partial(mix_kernel, so_far is None), grid_spec=p...  19.1 us
    select_n x5, other arithmetic, on_device(): jnp.where(core == 1, below, above)  6.31 us
  transfers between devices with their start and end apart: 48, of which 9 were waited for; matrix products, arithmetic and copies ran while one was open for 6% of the time, Pallas kernels for 33%

profile of v2, /device:TPU:0, one launch (start us, length us, event | category | flops | bytes accessed | tf_op | source)
XLA Modules:
  0.0 258.4 jit_solution(5527104456610123400)
XLA Ops:
  0.0 1.1 split.6
  1.1 3.0 %collective-permute-start = (bf16[192,1536]{1,0:T(8,128)(2,1)S(1)}, bf16[192,1536]{1,0:T(8,128)(2,1)S(1)}, u32[]{:S(2)}, u32[]{:S(2)}) collective-permute-start(bf16[192,1536]{1,0:T(8,128)(2,1)S(1)} %split.6), channel_id=1, source_target_pairs={{0,1},{1,0},{2,3},{3,2},{4,5},{5,4},{6,7},{7,6},{8,9},{9,8},{10,11... | collective-permute-start | bytes 1769480 | tf_op jit(solution)/shard_map/ppermute | solution.py:188
  4.1 13.3 %collective-permute-done = bf16[192,1536]{1,0:T(8,128)(2,1)S(1)} collective-permute-done((bf16[192,1536]{1,0:T(8,128)(2,1)S(1)}, bf16[192,1536]{1,0:T(8,128)(2,1)S(1)}, u32[]{:S(2)}, u32[]{:S(2)}) %collective-permute-start) | collective-permute-done | bytes 589856 | tf_op jit(solution)/shard_map/ppermute | solution.py:188
  17.5 2.2 broadcast_select_fusion.5
  19.6 5.5 %project.9.refs_0_ = bf16[2,192,512]{2,1,0:T(8,128)(2,1)} custom-call(bf16[192,1536]{1,0:T(8,128)(2,1)S(1)} %get-tuple-element.30.low_ref, bf16[192,1536]{1,0:T(8,128)(2,1)S(1)} %get-tuple-element.29.high_ref, bf16[3,3072,1536]{2,1,0:T(8,128)(2,1)} %bitcast.20, f32[1,128]{1,0:T(1,128)S(1)} %bitcast.14), custom_call_target="tpu_custom_call" | custom-call | flops 1207959552 | bytes 7864320 | tf_op jit(solution)/shard_map/project/pallas_call | solution.py:49
  25.2 1.8 collective-permute-start.6
  27.0 2.0 collective-permute-start.8
  29.0 1.7 collective-permute-start.1
  30.7 1.5 collective-permute-start.10
  32.3 7.0 %collective-permute-done.6.refs_2_ = bf16[2,192,512]{2,1,0:T(8,128)(2,1)S(1)} collective-permute-done((bf16[2,192,512]{2,1,0:T(8,128)(2,1)}, bf16[2,192,512]{2,1,0:T(8,128)(2,1)S(1)}, u32[]{:S(2)}, u32[]{:S(2)}) %collective-permute-start.6) | collective-permute-done | bytes 393248 | tf_op jit(solution)/shard_map/ppermute | solution.py:188
  39.3 6.0 %collective-permute-done.8.refs_4_ = bf16[2,192,512]{2,1,0:T(8,128)(2,1)S(1)} collective-permute-done((bf16[2,192,512]{2,1,0:T(8,128)(2,1)}, bf16[2,192,512]{2,1,0:T(8,128)(2,1)S(1)}, u32[]{:S(2)}, u32[]{:S(2)}) %collective-permute-start.8) | collective-permute-done | bytes 393248 | tf_op jit(solution)/shard_map/ppermute | solution.py:188
  45.3 0.9 broadcast_select_fusion.11
  46.2 1.5 collective-permute-start.11
  47.7 1.1 broadcast_select_fusion.4
  49.1 4.8 %project.10.refs_1_ = bf16[2,192,512]{2,1,0:T(8,128)(2,1)S(1)} custom-call(bf16[192,1536]{1,0:T(8,128)(2,1)S(1)} %get-tuple-element.32.low_ref, bf16[192,1536]{1,0:T(8,128)(2,1)S(1)} %get-tuple-element.31.high_ref, bf16[3,3072,1536]{2,1,0:T(8,128)(2,1)} %bitcast.21, f32[1,128]{1,0:T(1,128)S(1)} %bitcast.15), custom_call_target="tpu_custom_call" | custom-call | flops 1207959552 | bytes 7864320 | tf_op jit(solution)/shard_map/project/pallas_call | solution.py:49
  53.9 1.2 collective-permute-start.7
  55.0 2.7 %collective-permute-start.9 = (bf16[2,192,512]{2,1,0:T(8,128)(2,1)S(1)}, bf16[2,192,512]{2,1,0:T(8,128)(2,1)}, u32[]{:S(2)}, u32[]{:S(2)}) collective-permute-start(bf16[2,192,512]{2,1,0:T(8,128)(2,1)S(1)} %project.10.refs_1_), channel_id=1, source_target_pairs={{0,24},{2,26},{4,28},{6,30},{8,0},{10,2},{12,4},{14,6},{16,8},{18,... | collective-permute-start | bytes 1179656 | tf_op jit(solution)/shard_map/ppermute | solution.py:188
  57.7 8.0 %project.6.q_ref = bf16[1,384,1536]{2,1,0:T(8,128)(2,1)S(1)} custom-call(bf16[384,1536]{1,0:T(8,128)(2,1)S(1)} %get-tuple-element.16.low_ref, bf16[384,1536]{1,0:T(8,128)(2,1)S(1)} %get-tuple-element.17.high_ref, bf16[3,3072,1536]{2,1,0:T(8,128)(2,1)} %bitcast.22, f32[1,128]{1,0:T(1,128)S(1)} %bitcast.19), custom_call_target="tpu_custom_call" | custom-call | flops 3623878656 | bytes 12976128 | tf_op jit(solution)/shard_map/project/pallas_call | solution.py:49
  65.8 3.6 %project.8.refs_0_ = bf16[2,384,256]{2,1,0:T(8,128)(2,1)S(1)} custom-call(bf16[384,1536]{1,0:T(8,128)(2,1)S(1)} %get-tuple-element.16.low_ref, bf16[384,1536]{1,0:T(8,128)(2,1)S(1)} %get-tuple-element.17.high_ref, bf16[3,3072,1536]{2,1,0:T(8,128)(2,1)} %bitcast.23, f32[1,128]{1,0:T(1,128)S(1)} %bitcast.16), custom_call_target="tpu_custom_call" | custom-call | flops 1207959552 | bytes 5898240 | tf_op jit(solution)/shard_map/project/pallas_call | solution.py:49
  69.5 0.7 copy-done.12
  70.8 6.5 %project.11.refs_0_ = bf16[2,384,512]{2,1,0:T(8,128)(2,1)} custom-call(bf16[384,1536]{1,0:T(8,128)(2,1)S(1)} %get-tuple-element.16.low_ref, bf16[384,1536]{1,0:T(8,128)(2,1)S(1)} %get-tuple-element.17.high_ref, bf16[3,3072,1536]{2,1,0:T(8,128)(2,1)} %bitcast.24, f32[1,128]{1,0:T(1,128)S(1)} %bitcast.17), custom_call_target="tpu_custom_call" | custom-call | flops 2415919104 | bytes 9437184 | tf_op jit(solution)/shard_map/project/pallas_call | solution.py:49
  77.3 3.8 %collective-permute-start.25 = (bf16[2,384,512]{2,1,0:T(8,128)(2,1)}, bf16[2,384,512]{2,1,0:T(8,128)(2,1)}, u32[]{:S(2)}, u32[]{:S(2)}) collective-permute-start(bf16[2,384,512]{2,1,0:T(8,128)(2,1)} %project.11.refs_0_), channel_id=1, source_target_pairs={{0,24},{2,26},{4,28},{6,30},{8,0},{10,2},{12,4},{14,6},{16,8},{18,... | collective-permute-start | bytes 2359304 | tf_op jit(solution)/shard_map/ppermute | solution.py:188
  81.2 0.6 dynamic_slice.11
  81.8 2.1 broadcast_select_fusion.10
  83.8 2.1 collective-permute-start.5
  86.0 0.5 collective-permute-start.12
  86.5 1.5 collective-permute-start.13
  88.0 0.6 iota_compare_fusion
  89.1 1.9 dynamic_slice.12
  91.0 34.9 %collective-permute-done.5.refs_2_ = bf16[2,384,256]{2,1,0:T(8,128)(2,1)} collective-permute-done((bf16[2,384,256]{2,1,0:T(8,128)(2,1)S(1)}, bf16[2,384,256]{2,1,0:T(8,128)(2,1)}, u32[]{:S(2)}, u32[]{:S(2)}) %collective-permute-start.5) | collective-permute-done | bytes 393248 | tf_op jit(solution)/shard_map/ppermute | solution.py:188
  127.1 1.2 broadcast_select_fusion.8
  128.2 2.1 broadcast_select_fusion.2
  130.4 1.5 collective-permute-start.43
  131.9 0.5 collective-permute-start.26
  132.4 1.5 collective-permute-start.27
  133.9 0.7 copy-done.19
  134.6 0.8 copy-done.20
  135.4 18.3 %attend.4.own_ref = bf16[384,512]{1,0:T(8,128)(2,1)S(1)} custom-call(s32[9]{0:T(128)S(1)} %convert_element_type.3.used_ref, bf16[1,384,1536]{2,1,0:T(8,128)(2,1)} %copy-done.2, bf16[2,192,512]{2,1,0:T(8,128)(2,1)} %project.9.refs_0_, bf16[2,192,512]{2,1,0:T(8,128)(2,1)S(1)} %copy-done.5, bf16[2,192,512]{2,1,0:T(8,128)(2,1)S(1)} %copy-done.7, ...), custom_call_target="tpu_custom_call" | custom-call | flops 16307453952 | bytes 7864320 | tf_op jit(solution)/shard_map/attend/pallas_call | solution.py:117
  153.8 23.1 %collective-permute-done.22.refs_4_ = bf16[2,384,256]{2,1,0:T(8,128)(2,1)S(1)} collective-permute-done((bf16[2,384,256]{2,1,0:T(8,128)(2,1)S(1)}, bf16[2,384,256]{2,1,0:T(8,128)(2,1)S(1)}, u32[]{:S(2)}, u32[]{:S(2)}) %collective-permute-start.22) | collective-permute-done | bytes 393248 | tf_op jit(solution)/shard_map/ppermute | solution.py:188
  177.0 0.5 collective-permute-start.30
  177.5 3.2 %project.7.refs_0_ = bf16[2,384,256]{2,1,0:T(8,128)(2,1)S(1)} custom-call(bf16[384,1536]{1,0:T(8,128)(2,1)S(1)} %get-tuple-element.16.low_ref, bf16[384,1536]{1,0:T(8,128)(2,1)S(1)} %get-tuple-element.17.high_ref, bf16[3,3072,1536]{2,1,0:T(8,128)(2,1)} %bitcast.25, f32[1,128]{1,0:T(1,128)S(1)} %bitcast.18), custom_call_target="tpu_custom_call" | custom-call | flops 1207959552 | bytes 5898240 | tf_op jit(solution)/shard_map/project/pallas_call | solution.py:49
  180.8 0.7 collective-permute-start.2
  181.5 3.4 %collective-permute-start.3 = (bf16[2,384,256]{2,1,0:T(8,128)(2,1)S(1)}, bf16[2,384,256]{2,1,0:T(8,128)(2,1)S(1)}, u32[]{:S(2)}, u32[]{:S(2)}) collective-permute-start(bf16[2,384,256]{2,1,0:T(8,128)(2,1)S(1)} %project.7.refs_0_), channel_id=1, source_target_pairs={{0,24},{2,26},{4,28},{6,30},{8,0},{10,2},{12,4},{14,6},{16,8},{18,... | collective-permute-start | bytes 1179656 | tf_op jit(solution)/shard_map/ppermute | solution.py:188
  184.9 0.6 collective-permute-start.36
  186.3 13.6 %attend.5.own_ref = bf16[384,512]{1,0:T(8,128)(2,1)S(1)} custom-call(s32[9]{0:T(128)S(1)} %convert_element_type.3.used_ref, bf16[1,384,1536]{2,1,0:T(8,128)(2,1)} %copy-done.2, bf16[2,384,512]{2,1,0:T(8,128)(2,1)} %project.11.refs_0_, bf16[2,384,512]{2,1,0:T(8,128)(2,1)S(1)} %collective-permute-done.24.refs_1_, ...), custom_call_target="tpu_custom_call" | custom-call | flops 16307453952 | bytes 7864320 | tf_op jit(solution)/shard_map/attend/pallas_call | solution.py:117
  200.0 1.3 collective-permute-done.3.refs_2_
  201.2 0.5 collective-permute-start.23
  201.8 0.5 collective-permute-start.40
  202.5 9.1 %collective-permute-done.23.refs_3_ = bf16[2,384,256]{2,1,0:T(8,128)(2,1)S(1)} collective-permute-done((bf16[2,384,256]{2,1,0:T(8,128)(2,1)S(1)}, bf16[2,384,256]{2,1,0:T(8,128)(2,1)S(1)}, u32[]{:S(2)}, u32[]{:S(2)}) %collective-permute-start.23) | collective-permute-done | bytes 393248 | tf_op jit(solution)/shard_map/ppermute | solution.py:188
  211.6 0.5 collective-permute-start.35
  212.1 0.5 collective-permute-start.32
  212.6 7.7 %attend.6.own_ref = bf16[384,256]{1,0:T(8,128)(2,1)S(1)} custom-call(s32[9]{0:T(128)S(1)} %convert_element_type.3.used_ref, bf16[1,384,1536]{2,1,0:T(8,128)(2,1)S(1)} %copy-done.3, bf16[2,384,256]{2,1,0:T(8,128)(2,1)S(1)} %project.8.refs_0_, bf16[2,384,256]{2,1,0:T(8,128)(2,1)} %collective-permute-done.4.refs_1_, ...), custom_call_target="tpu_custom_call" | custom-call | flops 8153726976 | bytes 3932160 | tf_op jit(solution)/shard_map/attend/pallas_call | solution.py:117
  220.3 2.9 %collective-permute-done.32.refs_4_ = bf16[2,384,256]{2,1,0:T(8,128)(2,1)S(1)} collective-permute-done((bf16[2,384,256]{2,1,0:T(8,128)(2,1)S(1)}, bf16[2,384,256]{2,1,0:T(8,128)(2,1)S(1)}, u32[]{:S(2)}, u32[]{:S(2)}) %collective-permute-start.32) | collective-permute-done | bytes 393248 | tf_op jit(solution)/shard_map/ppermute | solution.py:188
  223.2 0.5 collective-permute-start.47
  223.8 1.5 collective-permute-start.46
  225.3 0.5 collective-permute-start.45
  225.8 6.3 %attend.7.own_ref = bf16[384,256]{1,0:T(8,128)(2,1)S(1)} custom-call(s32[9]{0:T(128)S(1)} %convert_element_type.3.used_ref, bf16[1,384,1536]{2,1,0:T(8,128)(2,1)S(1)} %copy-done.3, bf16[2,384,256]{2,1,0:T(8,128)(2,1)S(1)} %project.7.refs_0_, bf16[2,384,256]{2,1,0:T(8,128)(2,1)S(1)} %collective-permute-done.2.refs_1_, ...), custom_call_target="tpu_custom_call" | custom-call | flops 8153726976 | bytes 3932160 | tf_op jit(solution)/shard_map/attend/pallas_call | solution.py:117
  232.1 1.5 collective-permute-start.42
  233.7 2.3 broadcast_select_fusion.1
  235.9 2.5 pad_maximum_fusion.w_other
  238.4 4.8 %mix.4.refs_0_ = f32[384,1536]{1,0:T(8,128)S(1)} custom-call(s32[1]{0:T(128)} %bitcast.side_ref, bf16[384,512]{1,0:T(8,128)(2,1)S(1)} %attend.4.own_ref, bf16[384,512]{1,0:T(8,128)(2,1)S(1)} %collective-permute-done.47.other_ref, bf16[1536,3072]{1,0:T(8,128)(2,1)} %w_own.7, bf16[1536,1536]{1,0:T(8,128)(2,1)} %pad_maximum_fusion.w_other), custom_call_target="tpu_custom_call" | custom-call | flops 1207959552 | bytes 3145728 | tf_op jit(solution)/shard_map/mix/pallas_call | solution.py:159
  243.6 4.9 %mix.5.refs_0_ = f32[384,1536]{1,0:T(8,128)S(1)} custom-call(s32[1]{0:T(128)} %bitcast.side_ref, bf16[384,512]{1,0:T(8,128)(2,1)S(1)} %attend.5.own_ref, bf16[384,512]{1,0:T(8,128)(2,1)S(1)} %collective-permute-done.46.other_ref, bf16[1536,3072]{1,0:T(8,128)(2,1)} %w_own.7, bf16[1536,1536]{1,0:T(8,128)(2,1)} %pad_maximum_fusion.w_other, ...), custom_call_target="tpu_custom_call" | custom-call | flops 1207959552 | bytes 3145728 | tf_op jit(solution)/shard_map/mix/pallas_call | solution.py:159
  248.4 4.2 %mix.6.refs_0_ = f32[384,1536]{1,0:T(8,128)S(1)} custom-call(s32[1]{0:T(128)} %bitcast.side_ref, bf16[384,256]{1,0:T(8,128)(2,1)S(1)} %attend.6.own_ref, bf16[384,256]{1,0:T(8,128)(2,1)S(1)} %collective-permute-done.45.other_ref, bf16[1536,3072]{1,0:T(8,128)(2,1)} %w_own.7, bf16[1536,1536]{1,0:T(8,128)(2,1)} %pad_maximum_fusion.w_other, ...), custom_call_target="tpu_custom_call" | custom-call | flops 603979776 | bytes 1572864 | tf_op jit(solution)/shard_map/mix/pallas_call | solution.py:159
  252.7 5.2 %mix.7 = bf16[384,1536]{1,0:T(8,128)(2,1)} custom-call(s32[1]{0:T(128)} %bitcast.side_ref, bf16[384,256]{1,0:T(8,128)(2,1)S(1)} %attend.7.own_ref, bf16[384,256]{1,0:T(8,128)(2,1)S(1)} %collective-permute-done.42.other_ref, bf16[1536,3072]{1,0:T(8,128)(2,1)} %w_own.7, bf16[1536,1536]{1,0:T(8,128)(2,1)} %pad_maximum_fusion.w_other, f32[384,1536]{1,0:T(8,128)S(1)} %mix.6.refs_0_), custom_call_target="tpu_custom_call" | custom-call | flops 603979776 | bytes 1572864 | tf_op jit(solution)/shard_map/mix/pallas_call | solution.py:159
  (109 shorter events, 4.2 us)
Async XLA Ops:
  0.0 88.6 %copy-start = (s32[16,6]{0,1:T(8,128)S(1)}, s32[16,6]{0,1:T(8,128)}, u32[]{:S(2)}) copy-start(s32[16,6]{0,1:T(8,128)} %param.12) | copy-start | bytes 1156
  0.0 19.6 %copy-start.10 = (f32[128]{0:T(128)S(1)}, f32[128]{0:T(128)}, u32[]{:S(2)}) copy-start(f32[128]{0:T(128)} %param.10) | copy-start | bytes 1540
  1.1 16.3 %collective-permute-start = (bf16[192,1536]{1,0:T(8,128)(2,1)S(1)}, bf16[192,1536]{1,0:T(8,128)(2,1)S(1)}, u32[]{:S(2)}, u32[]{:S(2)}) collective-permute-start(bf16[192,1536]{1,0:T(8,128)(2,1)S(1)} %split.6), channel_id=1, source_target_pairs={{0,1},{1,0},{2,3},{3,2},{4,5},{5,4},{6,7},{7,6},{8,9},{9,8},{10,11... | collective-permute-start | bytes 1769480 | tf_op jit(solution)/shard_map/ppermute | solution.py:188
  19.6 28.1 %copy-start.14 = (bf16[384,1536]{1,0:T(8,128)(2,1)S(1)}, bf16[384,1536]{1,0:T(8,128)(2,1)}, u32[]{:S(2)}) copy-start(bf16[384,1536]{1,0:T(8,128)(2,1)} %param.7) | copy-start | bytes 3538948
  25.2 14.1 %collective-permute-start.6 = (bf16[2,192,512]{2,1,0:T(8,128)(2,1)}, bf16[2,192,512]{2,1,0:T(8,128)(2,1)S(1)}, u32[]{:S(2)}, u32[]{:S(2)}) collective-permute-start(bf16[2,192,512]{2,1,0:T(8,128)(2,1)} %project.9.refs_0_), channel_id=1, source_target_pairs={{0,8},{2,10},{4,12},{6,14},{8,16},{10,18},{12,20},{14,22},{16,24},... | collective-permute-start | bytes 1179656 | tf_op jit(solution)/shard_map/ppermute | solution.py:188
  27.0 18.3 %collective-permute-start.8 = (bf16[2,192,512]{2,1,0:T(8,128)(2,1)}, bf16[2,192,512]{2,1,0:T(8,128)(2,1)S(1)}, u32[]{:S(2)}, u32[]{:S(2)}) collective-permute-start(bf16[2,192,512]{2,1,0:T(8,128)(2,1)} %project.9.refs_0_), channel_id=1, source_target_pairs={{0,24},{2,26},{4,28},{6,30},{8,0},{10,2},{12,4},{14,6},{16,8},{18,... | collective-permute-start | bytes 1179656 | tf_op jit(solution)/shard_map/ppermute | solution.py:188
  29.0 18.7 %collective-permute-start.1 = (bf16[192,1536]{1,0:T(8,128)(2,1)}, bf16[192,1536]{1,0:T(8,128)(2,1)}, u32[]{:S(2)}, u32[]{:S(2)}) collective-permute-start(bf16[192,1536]{1,0:T(8,128)(2,1)} %get-tuple-element.35), channel_id=1, source_target_pairs={{0,1},{1,0},{2,3},{3,2},{4,5},{5,4},{6,7},{7,6},{8,9},{9,8},{10,11... | collective-permute-start | bytes 1769480 | tf_op jit(solution)/shard_map/ppermute | solution.py:188
  30.7 38.7 %collective-permute-start.10 = (bf16[2,192,512]{2,1,0:T(8,128)(2,1)}, bf16[2,192,512]{2,1,0:T(8,128)(2,1)}, u32[]{:S(2)}, u32[]{:S(2)}) collective-permute-start(bf16[2,192,512]{2,1,0:T(8,128)(2,1)} %project.9.refs_0_), channel_id=1, source_target_pairs={{0,4},{2,6},{4,0},{6,2},{8,12},{10,14},{12,8},{14,10},{16,20},{18,... | collective-permute-start | bytes 1179656 | tf_op jit(solution)/shard_map/ppermute | solution.py:188
  32.2 37.3 %collective-permute-start.14 = (bf16[2,192,512]{2,1,0:T(8,128)(2,1)}, bf16[2,192,512]{2,1,0:T(8,128)(2,1)S(1)}, u32[]{:S(2)}, u32[]{:S(2)}) collective-permute-start(bf16[2,192,512]{2,1,0:T(8,128)(2,1)} %project.9.refs_0_), channel_id=1, source_target_pairs={{0,2},{2,0},{4,6},{6,4},{8,10},{10,8},{12,14},{14,12},{16,18},{18,... | collective-permute-start | bytes 1179656 | tf_op jit(solution)/shard_map/ppermute | solution.py:188
  39.3 9.6 %copy-start.6 = (bf16[2,192,512]{2,1,0:T(8,128)(2,1)}, bf16[2,192,512]{2,1,0:T(8,128)(2,1)S(1)}, u32[]{:S(2)}) copy-start(bf16[2,192,512]{2,1,0:T(8,128)(2,1)S(1)} %collective-permute-done.6.refs_2_) | copy-start | bytes 1179652
  45.3 3.6 %copy-start.8 = (bf16[2,192,512]{2,1,0:T(8,128)(2,1)}, bf16[2,192,512]{2,1,0:T(8,128)(2,1)S(1)}, u32[]{:S(2)}) copy-start(bf16[2,192,512]{2,1,0:T(8,128)(2,1)S(1)} %collective-permute-done.8.refs_4_) | copy-start | bytes 1179652
  46.2 24.6 %collective-permute-start.11 = (bf16[2,192,512]{2,1,0:T(8,128)(2,1)S(1)}, bf16[2,192,512]{2,1,0:T(8,128)(2,1)}, u32[]{:S(2)}, u32[]{:S(2)}) collective-permute-start(bf16[2,192,512]{2,1,0:T(8,128)(2,1)S(1)} %get-tuple-element.43), channel_id=1, source_target_pairs={{0,4},{2,6},{4,0},{6,2},{8,12},{10,14},{12,8},{14,10},{16,20},{18,... | collective-permute-start | bytes 1179656 | tf_op jit(solution)/shard_map/ppermute | solution.py:188
  49.1 8.7 %copy-start.11 = (f32[128]{0:T(128)S(1)}, f32[128]{0:T(128)}, u32[]{:S(2)}) copy-start(f32[128]{0:T(128)} %param.9) | copy-start | bytes 1540
  53.9 11.9 %copy-start.4 = (bf16[2,192,512]{2,1,0:T(8,128)(2,1)}, bf16[2,192,512]{2,1,0:T(8,128)(2,1)S(1)}, u32[]{:S(2)}) copy-start(bf16[2,192,512]{2,1,0:T(8,128)(2,1)S(1)} %project.10.refs_1_) | copy-start | bytes 1179652
  53.9 23.4 %collective-permute-start.7 = (bf16[2,192,512]{2,1,0:T(8,128)(2,1)S(1)}, bf16[2,192,512]{2,1,0:T(8,128)(2,1)}, u32[]{:S(2)}, u32[]{:S(2)}) collective-permute-start(bf16[2,192,512]{2,1,0:T(8,128)(2,1)S(1)} %project.10.refs_1_), channel_id=1, source_target_pairs={{0,8},{2,10},{4,12},{6,14},{8,16},{10,18},{12,20},{14,22},{16,24},... | collective-permute-start | bytes 1179656 | tf_op jit(solution)/shard_map/ppermute | solution.py:188
  55.0 22.3 %collective-permute-start.9 = (bf16[2,192,512]{2,1,0:T(8,128)(2,1)S(1)}, bf16[2,192,512]{2,1,0:T(8,128)(2,1)}, u32[]{:S(2)}, u32[]{:S(2)}) collective-permute-start(bf16[2,192,512]{2,1,0:T(8,128)(2,1)S(1)} %project.10.refs_1_), channel_id=1, source_target_pairs={{0,24},{2,26},{4,28},{6,30},{8,0},{10,2},{12,4},{14,6},{16,8},{18,... | collective-permute-start | bytes 1179656 | tf_op jit(solution)/shard_map/ppermute | solution.py:188
  65.7 3.7 %copy-start.2 = (bf16[1,384,1536]{2,1,0:T(8,128)(2,1)}, bf16[1,384,1536]{2,1,0:T(8,128)(2,1)S(1)}, u32[]{:S(2)}) copy-start(bf16[1,384,1536]{2,1,0:T(8,128)(2,1)S(1)} %project.6.q_ref) | copy-start | bytes 3538948
  69.4 11.7 %copy-start.21 = (s32[16]{0:T(128)S(1)}, s32[16]{0:T(128)}, u32[]{:S(2)}) copy-start(s32[16]{0:T(128)} %param.13) | copy-start | bytes 196
  69.4 14.4 %collective-permute-start.16 = (bf16[2,192,512]{2,1,0:T(8,128)(2,1)}, bf16[2,192,512]{2,1,0:T(8,128)(2,1)}, u32[]{:S(2)}, u32[]{:S(2)}) collective-permute-start(bf16[2,192,512]{2,1,0:T(8,128)(2,1)} %get-tuple-element.42), channel_id=1, source_target_pairs={{0,2},{2,0},{4,6},{6,4},{8,10},{10,8},{12,14},{14,12},{16,18},{18,... | collective-permute-start | bytes 1179656 | tf_op jit(solution)/shard_map/ppermute | solution.py:188
  70.3 15.7 %collective-permute-start.18 = (bf16[2,192,512]{2,1,0:T(8,128)(2,1)}, bf16[2,192,512]{2,1,0:T(8,128)(2,1)}, u32[]{:S(2)}, u32[]{:S(2)}) collective-permute-start(bf16[2,192,512]{2,1,0:T(8,128)(2,1)} %collective-permute-done.10.refs_6_), channel_id=1, source_target_pairs={{0,2},{2,0},{4,6},{6,4},{8,10},{10,8},{12,14},{14,12},{16,18},{18,... | collective-permute-start | bytes 1179656 | tf_op jit(solution)/shard_map/ppermute | solution.py:188
  70.8 15.7 %collective-permute-start.4 = (bf16[2,384,256]{2,1,0:T(8,128)(2,1)S(1)}, bf16[2,384,256]{2,1,0:T(8,128)(2,1)}, u32[]{:S(2)}, u32[]{:S(2)}) collective-permute-start(bf16[2,384,256]{2,1,0:T(8,128)(2,1)S(1)} %project.8.refs_0_), channel_id=1, source_target_pairs={{0,8},{2,10},{4,12},{6,14},{8,16},{10,18},{12,20},{14,22},{16,24},... | collective-permute-start | bytes 1179656 | tf_op jit(solution)/shard_map/ppermute | solution.py:188
  77.3 49.2 %collective-permute-start.24 = (bf16[2,384,512]{2,1,0:T(8,128)(2,1)}, bf16[2,384,512]{2,1,0:T(8,128)(2,1)S(1)}, u32[]{:S(2)}, u32[]{:S(2)}) collective-permute-start(bf16[2,384,512]{2,1,0:T(8,128)(2,1)} %project.11.refs_0_), channel_id=1, source_target_pairs={{0,8},{2,10},{4,12},{6,14},{8,16},{10,18},{12,20},{14,22},{16,24},... | collective-permute-start | bytes 2359304 | tf_op jit(solution)/shard_map/ppermute | solution.py:188
  77.3 49.6 %collective-permute-start.25 = (bf16[2,384,512]{2,1,0:T(8,128)(2,1)}, bf16[2,384,512]{2,1,0:T(8,128)(2,1)}, u32[]{:S(2)}, u32[]{:S(2)}) collective-permute-start(bf16[2,384,512]{2,1,0:T(8,128)(2,1)} %project.11.refs_0_), channel_id=1, source_target_pairs={{0,24},{2,26},{4,28},{6,30},{8,0},{10,2},{12,4},{14,6},{16,8},{18,... | collective-permute-start | bytes 2359304 | tf_op jit(solution)/shard_map/ppermute | solution.py:188
  83.8 42.0 %collective-permute-start.5 = (bf16[2,384,256]{2,1,0:T(8,128)(2,1)S(1)}, bf16[2,384,256]{2,1,0:T(8,128)(2,1)}, u32[]{:S(2)}, u32[]{:S(2)}) collective-permute-start(bf16[2,384,256]{2,1,0:T(8,128)(2,1)S(1)} %project.8.refs_0_), channel_id=1, source_target_pairs={{0,24},{2,26},{4,28},{6,30},{8,0},{10,2},{12,4},{14,6},{16,8},{18,... | collective-permute-start | bytes 1179656 | tf_op jit(solution)/shard_map/ppermute | solution.py:188
  86.0 39.9 %collective-permute-start.12 = (bf16[2,192,512]{2,1,0:T(8,128)(2,1)}, bf16[2,192,512]{2,1,0:T(8,128)(2,1)}, u32[]{:S(2)}, u32[]{:S(2)}) collective-permute-start(bf16[2,192,512]{2,1,0:T(8,128)(2,1)} %copy-done.4), channel_id=1, source_target_pairs={{0,4},{2,6},{4,0},{6,2},{8,12},{10,14},{12,8},{14,10},{16,20},{18,... | collective-permute-start | bytes 1179656 | tf_op jit(solution)/shard_map/ppermute | solution.py:188
  86.5 39.9 %collective-permute-start.13 = (bf16[2,192,512]{2,1,0:T(8,128)(2,1)}, bf16[2,192,512]{2,1,0:T(8,128)(2,1)}, u32[]{:S(2)}, u32[]{:S(2)}) collective-permute-start(bf16[2,192,512]{2,1,0:T(8,128)(2,1)} %get-tuple-element.41), channel_id=1, source_target_pairs={{0,4},{2,6},{4,0},{6,2},{8,12},{10,14},{12,8},{14,10},{16,20},{18,... | collective-permute-start | bytes 1179656 | tf_op jit(solution)/shard_map/ppermute | solution.py:188
  89.0 36.8 %copy-start.5 = (bf16[2,192,512]{2,1,0:T(8,128)(2,1)S(1)}, bf16[2,192,512]{2,1,0:T(8,128)(2,1)}, u32[]{:S(2)}) copy-start(bf16[2,192,512]{2,1,0:T(8,128)(2,1)} %copy-done.4) | copy-start | bytes 1179652
  89.1 37.3 %copy-start.15 = (bf16[2,192,512]{2,1,0:T(8,128)(2,1)S(1)}, bf16[2,192,512]{2,1,0:T(8,128)(2,1)}, u32[]{:S(2)}) copy-start(bf16[2,192,512]{2,1,0:T(8,128)(2,1)} %get-tuple-element.40) | copy-start | bytes 1179652
  125.8 4.5 %collective-permute-start.15 = (bf16[2,192,512]{2,1,0:T(8,128)(2,1)S(1)}, bf16[2,192,512]{2,1,0:T(8,128)(2,1)S(1)}, u32[]{:S(2)}, u32[]{:S(2)}) collective-permute-start(bf16[2,192,512]{2,1,0:T(8,128)(2,1)S(1)} %copy-done.5), channel_id=1, source_target_pairs={{0,2},{2,0},{4,6},{6,4},{8,10},{10,8},{12,14},{14,12},{16,18},{18,... | collective-permute-start | bytes 1179656 | tf_op jit(solution)/shard_map/ppermute | solution.py:188
  125.9 6.0 %collective-permute-start.20 = (bf16[2,192,512]{2,1,0:T(8,128)(2,1)}, bf16[2,192,512]{2,1,0:T(8,128)(2,1)S(1)}, u32[]{:S(2)}, u32[]{:S(2)}) collective-permute-start(bf16[2,192,512]{2,1,0:T(8,128)(2,1)} %collective-permute-done.11.refs_8_), channel_id=1, source_target_pairs={{0,2},{2,0},{4,6},{6,4},{8,10},{10,8},{12,14},{14,12},{16,18},{18,... | collective-permute-start | bytes 1179656 | tf_op jit(solution)/shard_map/ppermute | solution.py:188
  126.4 9.0 %copy-start.7 = (bf16[2,192,512]{2,1,0:T(8,128)(2,1)S(1)}, bf16[2,192,512]{2,1,0:T(8,128)(2,1)}, u32[]{:S(2)}) copy-start(bf16[2,192,512]{2,1,0:T(8,128)(2,1)} %copy-done.6) | copy-start | bytes 1179652
  126.4 9.0 %copy-start.9 = (bf16[2,192,512]{2,1,0:T(8,128)(2,1)S(1)}, bf16[2,192,512]{2,1,0:T(8,128)(2,1)}, u32[]{:S(2)}) copy-start(bf16[2,192,512]{2,1,0:T(8,128)(2,1)} %copy-done.8) | copy-start | bytes 1179652
  126.4 9.0 %copy-start.13 = (bf16[2,192,512]{2,1,0:T(8,128)(2,1)S(1)}, bf16[2,192,512]{2,1,0:T(8,128)(2,1)}, u32[]{:S(2)}) copy-start(bf16[2,192,512]{2,1,0:T(8,128)(2,1)} %copy-done.12) | copy-start | bytes 1179652
  126.4 6.0 %collective-permute-start.17 = (bf16[2,192,512]{2,1,0:T(8,128)(2,1)S(1)}, bf16[2,192,512]{2,1,0:T(8,128)(2,1)S(1)}, u32[]{:S(2)}, u32[]{:S(2)}) collective-permute-start(bf16[2,192,512]{2,1,0:T(8,128)(2,1)S(1)} %copy-done.15), channel_id=1, source_target_pairs={{0,2},{2,0},{4,6},{6,4},{8,10},{10,8},{12,14},{14,12},{16,18},{18,... | collective-permute-start | bytes 1179656 | tf_op jit(solution)/shard_map/ppermute | solution.py:188
  126.5 7.4 %collective-permute-start.19 = (bf16[2,192,512]{2,1,0:T(8,128)(2,1)}, bf16[2,192,512]{2,1,0:T(8,128)(2,1)S(1)}, u32[]{:S(2)}, u32[]{:S(2)}) collective-permute-start(bf16[2,192,512]{2,1,0:T(8,128)(2,1)} %collective-permute-done.12.refs_7_), channel_id=1, source_target_pairs={{0,2},{2,0},{4,6},{6,4},{8,10},{10,8},{12,14},{14,12},{16,18},{18,... | collective-permute-start | bytes 1179656 | tf_op jit(solution)/shard_map/ppermute | solution.py:188
  127.0 6.9 %collective-permute-start.21 = (bf16[2,192,512]{2,1,0:T(8,128)(2,1)}, bf16[2,192,512]{2,1,0:T(8,128)(2,1)S(1)}, u32[]{:S(2)}, u32[]{:S(2)}) collective-permute-start(bf16[2,192,512]{2,1,0:T(8,128)(2,1)} %collective-permute-done.13.refs_9_), channel_id=1, source_target_pairs={{0,2},{2,0},{4,6},{6,4},{8,10},{10,8},{12,14},{14,12},{16,18},{18,... | collective-permute-start | bytes 1179656 | tf_op jit(solution)/shard_map/ppermute | solution.py:188
  130.4 55.1 %collective-permute-start.43 = (bf16[768,1536]{1,0:T(8,128)(2,1)S(1)}, bf16[768,1536]{1,0:T(8,128)(2,1)}, u32[]{:S(2)}, u32[]{:S(2)}) collective-permute-start(bf16[768,1536]{1,0:T(8,128)(2,1)S(1)} %dynamic_slice.12), channel_id=1, source_target_pairs={{0,1},{1,0},{2,3},{3,2},{4,5},{5,4},{6,7},{7,6},{8,9},{9,8},{10,11... | collective-permute-start | bytes 7077896 | tf_op jit(solution)/shard_map/ppermute | solution.py:188
  131.9 45.1 %collective-permute-start.26 = (bf16[2,384,512]{2,1,0:T(8,128)(2,1)}, bf16[2,384,512]{2,1,0:T(8,128)(2,1)S(1)}, u32[]{:S(2)}, u32[]{:S(2)}) collective-permute-start(bf16[2,384,512]{2,1,0:T(8,128)(2,1)} %project.11.refs_0_), channel_id=1, source_target_pairs={{0,4},{2,6},{4,0},{6,2},{8,12},{10,14},{12,8},{14,10},{16,20},{18,... | collective-permute-start | bytes 2359304 | tf_op jit(solution)/shard_map/ppermute | solution.py:188
  132.4 45.1 %collective-permute-start.27 = (bf16[2,384,512]{2,1,0:T(8,128)(2,1)S(1)}, bf16[2,384,512]{2,1,0:T(8,128)(2,1)S(1)}, u32[]{:S(2)}, u32[]{:S(2)}) collective-permute-start(bf16[2,384,512]{2,1,0:T(8,128)(2,1)S(1)} %get-tuple-element.34), channel_id=1, source_target_pairs={{0,4},{2,6},{4,0},{6,2},{8,12},{10,14},{12,8},{14,10},{16,20},{18,... | collective-permute-start | bytes 2359304 | tf_op jit(solution)/shard_map/ppermute | solution.py:188
  153.7 23.3 %collective-permute-start.22 = (bf16[2,384,256]{2,1,0:T(8,128)(2,1)S(1)}, bf16[2,384,256]{2,1,0:T(8,128)(2,1)S(1)}, u32[]{:S(2)}, u32[]{:S(2)}) collective-permute-start(bf16[2,384,256]{2,1,0:T(8,128)(2,1)S(1)} %get-tuple-element.19), channel_id=1, source_target_pairs={{0,4},{2,6},{4,0},{6,2},{8,12},{10,14},{12,8},{14,10},{16,20},{18,... | collective-permute-start | bytes 1179656 | tf_op jit(solution)/shard_map/ppermute | solution.py:188
  153.8 27.0 %collective-permute-start.28 = (bf16[2,384,512]{2,1,0:T(8,128)(2,1)}, bf16[2,384,512]{2,1,0:T(8,128)(2,1)S(1)}, u32[]{:S(2)}, u32[]{:S(2)}) collective-permute-start(bf16[2,384,512]{2,1,0:T(8,128)(2,1)} %project.11.refs_0_), channel_id=1, source_target_pairs={{0,2},{2,0},{4,6},{6,4},{8,10},{10,8},{12,14},{14,12},{16,18},{18,... | collective-permute-start | bytes 2359304 | tf_op jit(solution)/shard_map/ppermute | solution.py:188
  177.0 4.5 %collective-permute-start.29 = (bf16[2,384,512]{2,1,0:T(8,128)(2,1)}, bf16[2,384,512]{2,1,0:T(8,128)(2,1)S(1)}, u32[]{:S(2)}, u32[]{:S(2)}) collective-permute-start(bf16[2,384,512]{2,1,0:T(8,128)(2,1)} %get-tuple-element.33), channel_id=1, source_target_pairs={{0,2},{2,0},{4,6},{6,4},{8,10},{10,8},{12,14},{14,12},{16,18},{18,... | collective-permute-start | bytes 2359304 | tf_op jit(solution)/shard_map/ppermute | solution.py:188
  177.0 7.9 %collective-permute-start.30 = (bf16[2,384,512]{2,1,0:T(8,128)(2,1)S(1)}, bf16[2,384,512]{2,1,0:T(8,128)(2,1)S(1)}, u32[]{:S(2)}, u32[]{:S(2)}) collective-permute-start(bf16[2,384,512]{2,1,0:T(8,128)(2,1)S(1)} %collective-permute-done.26.refs_3_), channel_id=1, source_target_pairs={{0,2},{2,0},{4,6},{6,4},{8,10},{10,8},{12,14},{14,12},{16,18},{18,... | collective-permute-start | bytes 2359304 | tf_op jit(solution)/shard_map/ppermute | solution.py:188
  177.5 7.4 %collective-permute-start.31 = (bf16[2,384,512]{2,1,0:T(8,128)(2,1)S(1)}, bf16[2,384,512]{2,1,0:T(8,128)(2,1)S(1)}, u32[]{:S(2)}, u32[]{:S(2)}) collective-permute-start(bf16[2,384,512]{2,1,0:T(8,128)(2,1)S(1)} %collective-permute-done.27.refs_4_), channel_id=1, source_target_pairs={{0,2},{2,0},{4,6},{6,4},{8,10},{10,8},{12,14},{14,12},{16,18},{18,... | collective-permute-start | bytes 2359304 | tf_op jit(solution)/shard_map/ppermute | solution.py:188
  180.8 31.9 %copy-start.3 = (bf16[1,384,1536]{2,1,0:T(8,128)(2,1)S(1)}, bf16[1,384,1536]{2,1,0:T(8,128)(2,1)}, u32[]{:S(2)}) copy-start(bf16[1,384,1536]{2,1,0:T(8,128)(2,1)} %copy-done.2) | copy-start | bytes 3538948
  180.8 19.1 %collective-permute-start.2 = (bf16[2,384,256]{2,1,0:T(8,128)(2,1)S(1)}, bf16[2,384,256]{2,1,0:T(8,128)(2,1)S(1)}, u32[]{:S(2)}, u32[]{:S(2)}) collective-permute-start(bf16[2,384,256]{2,1,0:T(8,128)(2,1)S(1)} %project.7.refs_0_), channel_id=1, source_target_pairs={{0,8},{2,10},{4,12},{6,14},{8,16},{10,18},{12,20},{14,22},{16,24},... | collective-permute-start | bytes 1179656 | tf_op jit(solution)/shard_map/ppermute | solution.py:188
  181.5 19.8 %collective-permute-start.3 = (bf16[2,384,256]{2,1,0:T(8,128)(2,1)S(1)}, bf16[2,384,256]{2,1,0:T(8,128)(2,1)S(1)}, u32[]{:S(2)}, u32[]{:S(2)}) collective-permute-start(bf16[2,384,256]{2,1,0:T(8,128)(2,1)S(1)} %project.7.refs_0_), channel_id=1, source_target_pairs={{0,24},{2,26},{4,28},{6,30},{8,0},{10,2},{12,4},{14,6},{16,8},{18,... | collective-permute-start | bytes 1179656 | tf_op jit(solution)/shard_map/ppermute | solution.py:188
  184.9 16.9 %collective-permute-start.37 = (bf16[2,384,256]{2,1,0:T(8,128)(2,1)S(1)}, bf16[2,384,256]{2,1,0:T(8,128)(2,1)S(1)}, u32[]{:S(2)}, u32[]{:S(2)}) collective-permute-start(bf16[2,384,256]{2,1,0:T(8,128)(2,1)S(1)} %project.8.refs_0_), channel_id=1, source_target_pairs={{0,2},{2,0},{4,6},{6,4},{8,10},{10,8},{12,14},{14,12},{16,18},{18,... | collective-permute-start | bytes 1179656 | tf_op jit(solution)/shard_map/ppermute | solution.py:188
  184.9 16.9 %collective-permute-start.36 = (bf16[2,384,256]{2,1,0:T(8,128)(2,1)S(1)}, bf16[2,384,256]{2,1,0:T(8,128)(2,1)S(1)}, u32[]{:S(2)}, u32[]{:S(2)}) collective-permute-start(bf16[2,384,256]{2,1,0:T(8,128)(2,1)S(1)} %project.8.refs_0_), channel_id=1, source_target_pairs={{0,4},{2,6},{4,0},{6,2},{8,12},{10,14},{12,8},{14,10},{16,20},{18,... | collective-permute-start | bytes 1179656 | tf_op jit(solution)/shard_map/ppermute | solution.py:188
  185.8 47.8 %collective-permute-start.44 = (bf16[768,1536]{1,0:T(8,128)(2,1)}, bf16[768,1536]{1,0:T(8,128)(2,1)S(1)}, u32[]{:S(2)}, u32[]{:S(2)}) collective-permute-start(bf16[768,1536]{1,0:T(8,128)(2,1)} %collective-permute-done.43), channel_id=1, source_target_pairs={{0,2},{2,0},{4,6},{6,4},{8,10},{10,8},{12,14},{14,12},{16,18},{18,... | collective-permute-start | bytes 7077896 | tf_op jit(solution)/shard_map/ppermute | solution.py:188
  199.9 2.4 collective-permute-start.38
  201.2 10.4 %collective-permute-start.23 = (bf16[2,384,256]{2,1,0:T(8,128)(2,1)S(1)}, bf16[2,384,256]{2,1,0:T(8,128)(2,1)S(1)}, u32[]{:S(2)}, u32[]{:S(2)}) collective-permute-start(bf16[2,384,256]{2,1,0:T(8,128)(2,1)S(1)} %project.7.refs_0_), channel_id=1, source_target_pairs={{0,4},{2,6},{4,0},{6,2},{8,12},{10,14},{12,8},{14,10},{16,20},{18,... | collective-permute-start | bytes 1179656 | tf_op jit(solution)/shard_map/ppermute | solution.py:188
  201.8 9.8 %collective-permute-start.39 = (bf16[2,384,256]{2,1,0:T(8,128)(2,1)S(1)}, bf16[2,384,256]{2,1,0:T(8,128)(2,1)S(1)}, u32[]{:S(2)}, u32[]{:S(2)}) collective-permute-start(bf16[2,384,256]{2,1,0:T(8,128)(2,1)S(1)} %collective-permute-done.36.refs_3_), channel_id=1, source_target_pairs={{0,2},{2,0},{4,6},{6,4},{8,10},{10,8},{12,14},{14,12},{16,18},{18,... | collective-permute-start | bytes 1179656 | tf_op jit(solution)/shard_map/ppermute | solution.py:188
  201.8 10.3 %collective-permute-start.40 = (bf16[2,384,256]{2,1,0:T(8,128)(2,1)S(1)}, bf16[2,384,256]{2,1,0:T(8,128)(2,1)S(1)}, u32[]{:S(2)}, u32[]{:S(2)}) collective-permute-start(bf16[2,384,256]{2,1,0:T(8,128)(2,1)S(1)} %collective-permute-done.22.refs_4_), channel_id=1, source_target_pairs={{0,2},{2,0},{4,6},{6,4},{8,10},{10,8},{12,14},{14,12},{16,18},{18,... | collective-permute-start | bytes 1179656 | tf_op jit(solution)/shard_map/ppermute | solution.py:188
  202.3 20.9 %collective-permute-start.33 = (bf16[2,384,256]{2,1,0:T(8,128)(2,1)S(1)}, bf16[2,384,256]{2,1,0:T(8,128)(2,1)S(1)}, u32[]{:S(2)}, u32[]{:S(2)}) collective-permute-start(bf16[2,384,256]{2,1,0:T(8,128)(2,1)S(1)} %project.7.refs_0_), channel_id=1, source_target_pairs={{0,2},{2,0},{4,6},{6,4},{8,10},{10,8},{12,14},{14,12},{16,18},{18,... | collective-permute-start | bytes 1179656 | tf_op jit(solution)/shard_map/ppermute | solution.py:188
  211.6 12.2 %collective-permute-start.34 = (bf16[2,384,256]{2,1,0:T(8,128)(2,1)S(1)}, bf16[2,384,256]{2,1,0:T(8,128)(2,1)S(1)}, u32[]{:S(2)}, u32[]{:S(2)}) collective-permute-start(bf16[2,384,256]{2,1,0:T(8,128)(2,1)S(1)} %get-tuple-element.38), channel_id=1, source_target_pairs={{0,2},{2,0},{4,6},{6,4},{8,10},{10,8},{12,14},{14,12},{16,18},{18,... | collective-permute-start | bytes 1179656 | tf_op jit(solution)/shard_map/ppermute | solution.py:188
  211.6 13.6 %collective-permute-start.35 = (bf16[2,384,256]{2,1,0:T(8,128)(2,1)S(1)}, bf16[2,384,256]{2,1,0:T(8,128)(2,1)S(1)}, u32[]{:S(2)}, u32[]{:S(2)}) collective-permute-start(bf16[2,384,256]{2,1,0:T(8,128)(2,1)S(1)} %collective-permute-done.23.refs_3_), channel_id=1, source_target_pairs={{0,2},{2,0},{4,6},{6,4},{8,10},{10,8},{12,14},{14,12},{16,18},{18,... | collective-permute-start | bytes 1179656 | tf_op jit(solution)/shard_map/ppermute | solution.py:188
  212.1 11.1 %collective-permute-start.32 = (bf16[2,384,256]{2,1,0:T(8,128)(2,1)S(1)}, bf16[2,384,256]{2,1,0:T(8,128)(2,1)S(1)}, u32[]{:S(2)}, u32[]{:S(2)}) collective-permute-start(bf16[2,384,256]{2,1,0:T(8,128)(2,1)S(1)} %get-tuple-element.22), channel_id=1, source_target_pairs={{0,4},{2,6},{4,0},{6,2},{8,12},{10,14},{12,8},{14,10},{16,20},{18,... | collective-permute-start | bytes 1179656 | tf_op jit(solution)/shard_map/ppermute | solution.py:188
  223.2 2.6 %collective-permute-start.41 = (bf16[2,384,256]{2,1,0:T(8,128)(2,1)S(1)}, bf16[2,384,256]{2,1,0:T(8,128)(2,1)S(1)}, u32[]{:S(2)}, u32[]{:S(2)}) collective-permute-start(bf16[2,384,256]{2,1,0:T(8,128)(2,1)S(1)} %collective-permute-done.32.refs_4_), channel_id=1, source_target_pairs={{0,2},{2,0},{4,6},{6,4},{8,10},{10,8},{12,14},{14,12},{16,18},{18,... | collective-permute-start | bytes 1179656 | tf_op jit(solution)/shard_map/ppermute | solution.py:188
  223.2 15.2 %collective-permute-start.47 = (bf16[384,512]{1,0:T(8,128)(2,1)S(1)}, bf16[384,512]{1,0:T(8,128)(2,1)S(1)}, u32[]{:S(2)}, u32[]{:S(2)}) collective-permute-start(bf16[384,512]{1,0:T(8,128)(2,1)S(1)} %attend.4.own_ref), channel_id=1, source_target_pairs={{0,1},{1,0},{2,3},{3,2},{4,5},{5,4},{6,7},{7,6},{8,9},{9,8},{10,11... | collective-permute-start | bytes 1179656 | tf_op jit(solution)/shard_map/ppermute | solution.py:188
  223.8 19.8 %collective-permute-start.46 = (bf16[384,512]{1,0:T(8,128)(2,1)S(1)}, bf16[384,512]{1,0:T(8,128)(2,1)S(1)}, u32[]{:S(2)}, u32[]{:S(2)}) collective-permute-start(bf16[384,512]{1,0:T(8,128)(2,1)S(1)} %attend.5.own_ref), channel_id=1, source_target_pairs={{0,1},{1,0},{2,3},{3,2},{4,5},{5,4},{6,7},{7,6},{8,9},{9,8},{10,11... | collective-permute-start | bytes 1179656 | tf_op jit(solution)/shard_map/ppermute | solution.py:188
  225.3 23.2 %collective-permute-start.45 = (bf16[384,256]{1,0:T(8,128)(2,1)S(1)}, bf16[384,256]{1,0:T(8,128)(2,1)S(1)}, u32[]{:S(2)}, u32[]{:S(2)}) collective-permute-start(bf16[384,256]{1,0:T(8,128)(2,1)S(1)} %attend.6.own_ref), channel_id=1, source_target_pairs={{0,1},{1,0},{2,3},{3,2},{4,5},{5,4},{6,7},{7,6},{8,9},{9,8},{10,11... | collective-permute-start | bytes 589832 | tf_op jit(solution)/shard_map/ppermute | solution.py:188
  232.1 20.6 %collective-permute-start.42 = (bf16[384,256]{1,0:T(8,128)(2,1)S(1)}, bf16[384,256]{1,0:T(8,128)(2,1)S(1)}, u32[]{:S(2)}, u32[]{:S(2)}) collective-permute-start(bf16[384,256]{1,0:T(8,128)(2,1)S(1)} %attend.7.own_ref), channel_id=1, source_target_pairs={{0,1},{1,0},{2,3},{3,2},{4,5},{5,4},{6,7},{7,6},{8,9},{9,8},{10,11... | collective-permute-start | bytes 589832 | tf_op jit(solution)/shard_map/ppermute | solution.py:188
  252.7 5.2 %copy-start.1 = (s32[16,6]{0,1:T(8,128)S(1)}, s32[16,6]{0,1:T(8,128)}, u32[]{:S(2)}) copy-start(s32[16,6]{0,1:T(8,128)} %param.12) | copy-start | bytes 1156
  (6 other events, 6.6 us)
